TPU v7x, 256 devices: a whole 4x4x8 slice. The times are simulated.
256 devices in a mesh: sfc: 64 (over y, z, core), aux: 4 (over x).
Axes of the slice: x: 4, y: 4, z: 8, core: 2. Of those that a mesh axis runs over, the one named last changes fastest.
Arguments:
- three_index: bfloat16 [128, 4, 160, 128, 128], P('sfc', None, 'aux'), may hold values from -0.14941406 to 0.14941406
- density: bfloat16 [128, 13, 128, 128], P('sfc'), may hold values from -6 to 6
- neighbours: int32 [128, 4], P('sfc'), may hold values from 0 to 127, as said below
- partner: int32 [128, 4], P('sfc'), may hold values from 0 to 3
- block_mask: int32 [128, 4], P('sfc'), may hold values 0 or 1
Outputs:
- exchange: float32 [128, 13, 128, 128], P('sfc', None, 'aux')
Inputs may be any that keep to these rules, and one draw needn't show every extreme that they name: neighbours[g, 0] is g; the entries of a row are distinct groups (g + s) mod 128 with s between -3 and 3.
All inputs are finite; a program needn't handle non-finite values. No bound on the sum of `block_mask` on one device may be relied on, other than what follows from the above.
Results may differ from a plain program's by a relative error of at most 0.0029.
Values may be sent and summed in bfloat16 or wider, within the bound.
No kernel may reach another device: no remote copies, remote signals or barrier semaphores. Data moves between devices by JAX's collectives and lax.ppermute only.
A program may use at most 128 MiB of HBM per device.

v0:
```python
import jax
import jax.numpy as jnp
from jax import lax
from jax.sharding import PartitionSpec as P

RANGE = 3


def passed_along(value, axis, steps):
    count = lax.axis_size(axis)
    pairs = [(source, (source + steps) % count) for source in range(count)]
    return lax.ppermute(value, axis, pairs)


def local(three_index, density, neighbours, partner, block_mask):
    group_dev, neigh = neighbours.shape
    offsets = density.shape[1]
    basis = density.shape[2]
    aux_dev = three_index.shape[2]
    center = (offsets - 1) // 2
    devices = lax.axis_size("sfc")
    total_groups = devices * group_dev
    reach = (RANGE + group_dev - 1) // group_dev
    span = 2 * reach + 1
    slots = group_dev * min(group_dev, neigh)
    count = group_dev * neigh
    band_slots = group_dev * offsets
    mine = lax.axis_index("sfc")
    highest = lax.Precision.HIGHEST
    other = jnp.take_along_axis(neighbours, partner, axis=1)
    offset = jnp.mod(other - neighbours + center, total_groups).reshape(count)
    weight = (
        (block_mask * jnp.take_along_axis(block_mask, partner, axis=1))
        .astype(jnp.float32)
        .reshape(count)
    )
    target = neighbours.reshape(count)
    order_ids = jnp.arange(count, dtype=jnp.int32)
    paired_index = order_ids // neigh * neigh + partner.reshape(count)
    owner = target // group_dev
    within = target % group_dev
    same_owner = owner[:, None] == owner[None, :]
    earlier = order_ids[None, :] < order_ids[:, None]
    rank = jnp.sum(jnp.logical_and(same_owner, earlier), axis=1)
    destination = within * offsets + offset
    relative = jnp.mod(owner - mine + reach, devices)
    packed_position = relative * slots + rank
    packed_table = packed_position[None, :] == jnp.arange(span * slots)[:, None]
    home_blocks = density[:, center]
    blocks = three_index.reshape(count, aux_dev, basis, basis)
    paired = jnp.take(blocks, paired_index, axis=0)
    paired_grouped = paired.reshape(group_dev, neigh, aux_dev, basis, basis)
    right = jnp.einsum(
        "gml,gjplc->gjpmc", home_blocks, paired_grouped, preferred_element_type=jnp.float32
    ).astype(jnp.bfloat16)
    right = right.reshape(count, aux_dev, basis, basis)
    cross = (
        jnp.einsum("jpmn,jpmc->jnc", blocks, right, preferred_element_type=jnp.float32)
        * weight[:, None, None]
    )
    requests = (jnp.sum(jnp.where(packed_table, destination[None, :] + 1, 0), axis=1) - 1).reshape(
        span, slots
    )
    flat_density = density.reshape(band_slots, basis, basis)
    replies = []
    for step in range(span):
        delta = step - reach
        if delta == 0:
            replies.append(flat_density[jnp.clip(requests[step], 0, band_slots - 1)])
        else:
            asked = passed_along(requests[step], "sfc", delta)
            found = flat_density[jnp.clip(asked, 0, band_slots - 1)]
            replies.append(passed_along(found, "sfc", -delta))
    far = jnp.stack(replies).reshape(span * slots, basis, basis)[packed_position]
    left = jnp.einsum("jac,jpmc->jpam", far, paired, preferred_element_type=jnp.float32).astype(
        jnp.bfloat16
    )
    own = (
        jnp.einsum("jpma,jpan->jmn", blocks, left, preferred_element_type=jnp.float32)
        * weight[:, None, None]
    )
    diagonal = jnp.sum(own.reshape(group_dev, neigh, basis, basis), axis=1)
    cross_part, diagonal_part = (
        lax.psum_scatter(cross, "aux", scatter_dimension=1, tiled=True),
        lax.psum_scatter(diagonal, "aux", scatter_dimension=1, tiled=True),
    )
    rows = cross_part.shape[1]
    outgoing = jnp.einsum(
        "qi,irc->qrc", packed_table.astype(jnp.float32), cross_part, precision=highest
    ).reshape(span, slots, rows, basis)
    labels = (jnp.sum(jnp.where(packed_table, destination[None, :] + 1, 0), axis=1) - 1).reshape(
        span, slots
    )
    arrived_all = []
    labels_all = []
    for step in range(span):
        delta = step - reach
        if delta == 0:
            arrived_all.append(outgoing[step])
            labels_all.append(labels[step])
        else:
            arrived, arrived_labels = passed_along((outgoing[step], labels[step]), "sfc", delta)
            arrived_all.append(arrived)
            labels_all.append(arrived_labels)
    flat_in = jnp.stack(arrived_all).reshape(span * slots, rows * basis)
    label_in = jnp.stack(labels_all).reshape(span * slots)
    table_in = (label_in[None, :] == jnp.arange(band_slots)[:, None]).astype(jnp.float32)
    summed = jnp.dot(table_in, flat_in, precision=highest)
    band = summed.reshape(group_dev, offsets, rows, basis)
    band = band.at[:, center].add(diagonal_part)
    return band


def solution(mesh):
    return jax.shard_map(
        local,
        mesh=mesh,
        in_specs=(
            P("sfc", None, "aux", None, None),
            P("sfc", None, None, None),
            P("sfc", None),
            P("sfc", None),
            P("sfc", None),
        ),
        out_specs=P("sfc", None, "aux", None),
        check_vma=False,
    )
```

profile of v0, /device:TPU:1, one launch (start us, length us, event | category | flops | bytes accessed | tf_op | source)
XLA Modules:
  0.0 125.6 jit_solution(5347679570627357941)
XLA Ops:
  6.5 0.8 reshape.409
  7.3 0.7 bitcast_or_fusion
  8.0 0.1 reshape.506
  8.1 1.3 %gather_fusion.7 = s32[8]{0:T(128)S(1)} fusion(s32[2,4]{1,0:T(2,128)} %param.11, s32[8]{0:T(128)S(1)} %reshape.506), kind=kCustom, calls=%fused_computation.clone | custom fusion | bytes 128 | tf_op jit(solution)/shard_map/jit(take_along_axis)/gather | solution.py:30
  9.4 1.3 %gather_fusion.8 = s32[8]{0:T(128)S(1)} fusion(s32[2,4]{1,0:T(2,128)} %param.13, s32[8]{0:T(128)S(1)} %reshape.506), kind=kCustom, calls=%fused_computation.1.clone | custom fusion | bytes 128 | tf_op jit(solution)/shard_map/jit(take_along_axis)/gather | solution.py:33
  10.9 0.7 and_select_fusion.5
  11.6 0.1 reshape.410
  11.7 0.2 convert_reduce_fusion
  11.9 0.1 select_reduce_fusion
  12.1 2.5 %collective-permute-start.3 = (s32[4]{0:T(128)S(1)}, s32[4]{0:T(128)S(1)}, u32[]{:S(2)}, u32[]{:S(2)}) collective-permute-start(s32[4]{0:T(128)S(1)} %get-tuple-element.25), channel_id=1, source_target_pairs={{0,8},{4,12},{8,16},{12,20},{16,24},{20,28},{24,32},{28,36},{32,40... | collective-permute-start | bytes 56 | tf_op jit(solution)/shard_map/ppermute | solution.py:12
  14.6 2.5 %collective-permute-start.2 = (s32[4]{0:T(128)S(1)}, s32[4]{0:T(128)S(1)}, u32[]{:S(2)}, u32[]{:S(2)}) collective-permute-start(s32[4]{0:T(128)S(1)} %get-tuple-element.26), channel_id=1, source_target_pairs={{0,4},{4,8},{8,12},{12,16},{16,20},{20,24},{24,28},{28,32},{32,36}... | collective-permute-start | bytes 56 | tf_op jit(solution)/shard_map/ppermute | solution.py:12
  17.1 4.8 %collective-permute-start = (s32[4]{0:T(128)S(1)}, s32[4]{0:T(128)S(1)}, u32[]{:S(2)}, u32[]{:S(2)}) collective-permute-start(s32[4]{0:T(128)S(1)} %get-tuple-element.29), channel_id=1, source_target_pairs={{0,248},{4,252},{8,0},{12,4},{16,8},{20,12},{24,16},{28,20},{32,24... | collective-permute-start | bytes 56 | tf_op jit(solution)/shard_map/ppermute | solution.py:12
  21.8 0.8 reshape.418
  22.6 0.7 compare_and_fusion.2
  23.3 0.8 reshape.412
  24.1 0.1 mul.70
  24.2 9.6 %gather_fusion = bf16[8,40,128,128]{3,2,1,0:T(8,128)(2,1)} fusion(bf16[8,40,128,128]{3,2,1,0:T(8,128)(2,1)} %bitcast.123, s32[1024]{0:T(1024)S(1)} %get-tuple-element.33), kind=kCustom, calls=%fused_computation.2 | custom fusion | bytes 20971552 | tf_op jit(solution)/shard_map/jit(_take)/gather | solution.py:51
  33.8 13.8 %copy.23 = bf16[2,4,40,128,128]{3,4,2,1,0:T(8,128)(2,1)} copy(bf16[2,4,40,128,128]{4,3,2,1,0:T(8,128)(2,1)} %bitcast.126) | data formatting | bytes 20971520 | tf_op jit(solution)/shard_map/jit(_take)/gather | solution.py:51
  47.6 5.7 %fusion.12 = bf16[2,4,40,128,128]{4,3,2,1,0:T(8,128)(2,1)S(1)} fusion(bf16[2,4,40,128,128]{3,4,2,1,0:T(8,128)(2,1)} %copy.23, pred[2,4]{1,0:T(4,128)(4,1)S(1)} %compare_and_fusion.2, bf16[2,13,128,128]{3,2,1,0:T(8,128)(2,1)S(1)} %copy-done), kind=kOutput, calls=%fused_computation.18 | convolution fusion | flops 1352663040 | bytes 21037568 | tf_op jit(solution)/shard_map/gml,gjplc->gjpmc/dot_general | solution.py:53
  53.3 5.7 %fusion.29 = f32[8,128,128]{1,2,0:T(8,128)S(1)} fusion(bf16[8,40,128,128]{2,3,1,0:T(8,128)(2,1)S(1)} %bitcast.127, bf16[8,40,128,128]{3,2,1,0:T(8,128)(2,1)} %bitcast.124, f32[8]{0:T(128)S(1)} %mul.70), kind=kOutput, calls=%fused_computation.25 | convolution fusion | flops 1342308352 | bytes 21495840 | tf_op jit(solution)/shard_map/jpmn,jpmc->jnc/dot_general | solution.py:58
  59.0 1.0 copy.25
  60.1 0.1 reshape.415
  60.2 0.6 gather_fusion.3
  60.9 0.6 gather_fusion.1
  61.5 0.1 collective-permute-start.8
  61.7 0.6 gather_fusion.2
  62.3 0.6 gather_fusion.5
  62.9 0.6 gather_fusion.4
  63.5 2.0 %collective-permute-start.10 = (bf16[4,128,128]{2,1,0:T(8,128)(2,1)S(1)}, bf16[4,128,128]{2,1,0:T(8,128)(2,1)S(1)}, u32[]{:S(2)}, u32[]{:S(2)}) collective-permute-start(bf16[4,128,128]{2,1,0:T(8,128)(2,1)S(1)} %gather_fusion.4), channel_id=1, source_target_pairs={{0,252},{4,0},{8,4},{12,8},{16,12},{20,16},{24,20},{28,24},{32,28}... | collective-permute-start | bytes 393224 | tf_op jit(solution)/shard_map/ppermute | solution.py:12
  65.5 5.1 %collective-permute-start.11 = (bf16[4,128,128]{2,1,0:T(8,128)(2,1)S(1)}, bf16[4,128,128]{2,1,0:T(8,128)(2,1)S(1)}, u32[]{:S(2)}, u32[]{:S(2)}) collective-permute-start(bf16[4,128,128]{2,1,0:T(8,128)(2,1)S(1)} %gather_fusion.5), channel_id=1, source_target_pairs={{0,248},{4,252},{8,0},{12,4},{16,8},{20,12},{24,16},{28,20},{32,24... | collective-permute-start | bytes 393224 | tf_op jit(solution)/shard_map/ppermute | solution.py:12
  70.5 1.9 %collective-permute-done.9 = bf16[4,128,128]{2,1,0:T(8,128)(2,1)S(1)} collective-permute-done((bf16[4,128,128]{2,1,0:T(8,128)(2,1)S(1)}, bf16[4,128,128]{2,1,0:T(8,128)(2,1)S(1)}, u32[]{:S(2)}, u32[]{:S(2)}) %collective-permute-start.9) | collective-permute-done | bytes 131104 | tf_op jit(solution)/shard_map/ppermute | solution.py:12
  72.6 0.8 collective-permute-done.11
  73.4 0.6 gather_fusion.6
  74.0 7.6 %reduce-scatter.3.cloned.1.call-done = f32[8,32,128]{2,0,1:T(8,128)} async-done(((f32[8,128,128]{2,0,1:T(8,128)}), f32[8,32,128]{2,0,1:T(8,128)}) %reduce-scatter.3.cloned.1.call-update) | async-done | bytes 131088 | tf_op jit(solution)/shard_map/reduce_scatter | solution.py:84
  81.6 1.3 %fusion.50 = f32[20,32,128]{2,0,1:T(8,128)S(1)} fusion(f32[8,32,128]{2,0,1:T(8,128)} %reduce-scatter.3.cloned.1.call-done, s32[8]{0:T(128)S(1)} %fusion.61), kind=kOutput, calls=%fused_computation.63 | convolution fusion | flops 7864480 | bytes 458784 | tf_op jit(solution)/shard_map/qi,irc->qrc/dot_general | solution.py:88
  82.9 5.5 %collective-permute-start.4 = (f32[4,32,128]{2,0,1:T(4,128)S(1)}, f32[4,32,128]{2,0,1:T(4,128)S(1)}, u32[]{:S(2)}, u32[]{:S(2)}) collective-permute-start(f32[4,32,128]{2,0,1:T(4,128)S(1)} %get-tuple-element.21), channel_id=1, source_target_pairs={{0,248},{4,252},{8,0},{12,4},{16,8},{20,12},{24,16},{28,20},{32,24... | collective-permute-start | bytes 196616 | tf_op jit(solution)/shard_map/ppermute | solution.py:12
  88.4 10.0 %bitcast_reduce_fusion = f32[2,128,128]{1,2,0:T(8,128)S(1)} fusion(bf16[8,40,128,128]{3,2,1,0:T(8,128)(2,1)} %bitcast.125, bf16[8,40,128,128]{3,2,1,0:T(8,128)(2,1)} %gather_fusion, pred[8]{0:T(512)(128)(4,1)S(1)} %compare_and_fusion.1, bf16[8,128,128]{2,1,0:T(8,128)(2,1)S(1)} %gather_fusion.6, f32[8]{0:T(128)S(1)} %mul.70), kind=kOutput, calls=%fused_computation.26 | convolution fusion | flops 2695069696 | bytes 21364776 | tf_op jit(solution)/shard_map/jpma,jpan->jmn/dot_general | solution.py:79
  98.5 0.8 copy.28
  99.3 0.1 collective-permute-start.7
  99.4 0.3 collective-permute-start.6
  99.6 2.5 %collective-permute-start.5 = (f32[4,32,128]{2,0,1:T(4,128)S(1)}, f32[4,32,128]{2,0,1:T(4,128)S(1)}, u32[]{:S(2)}, u32[]{:S(2)}) collective-permute-start(f32[4,32,128]{2,0,1:T(4,128)S(1)} %get-tuple-element.20), channel_id=1, source_target_pairs={{0,252},{4,0},{8,4},{12,8},{16,12},{20,16},{24,20},{28,24},{32,28}... | collective-permute-start | bytes 196616 | tf_op jit(solution)/shard_map/ppermute | solution.py:12
  102.1 1.2 collective-permute-done.5
  103.4 2.4 %collective-permute-done.7 = f32[4,32,128]{2,0,1:T(4,128)S(1)} collective-permute-done((f32[4,32,128]{2,0,1:T(4,128)S(1)}, f32[4,32,128]{2,0,1:T(4,128)S(1)}, u32[]{:S(2)}, u32[]{:S(2)}) %collective-permute-start.7) | collective-permute-done | bytes 65568 | tf_op jit(solution)/shard_map/ppermute | solution.py:12
  105.9 0.6 fusion.30
  106.4 10.5 %reduce-scatter.5.cloned.1.call-done = f32[2,32,128]{2,1,0:T(8,128)} async-done(((f32[2,128,128]{2,1,0:T(8,128)}), f32[2,32,128]{2,1,0:T(8,128)}) %reduce-scatter.5.cloned.1.call-update) | async-done | bytes 32784 | tf_op jit(solution)/shard_map/reduce_scatter | solution.py:85
  116.9 0.8 slice_add_fusion
  117.7 0.1 scatter-add.4
  117.9 0.9 copy.29
  (51 shorter events, 0.8 us)
Async XLA Ops:
  6.5 75.0 %reduce-scatter.3.cloned.1.call-start = ((), (), s32[]{:S(2)}) async-start(), calls=%async_computation.2 | async-start | bytes 655360 | tf_op jit(solution)/shard_map/reduce_scatter | solution.py:84
  12.1 49.4 %collective-permute-start.3 = (s32[4]{0:T(128)S(1)}, s32[4]{0:T(128)S(1)}, u32[]{:S(2)}, u32[]{:S(2)}) collective-permute-start(s32[4]{0:T(128)S(1)} %get-tuple-element.25), channel_id=1, source_target_pairs={{0,8},{4,12},{8,16},{12,20},{16,24},{20,28},{24,32},{28,36},{32,40... | collective-permute-start | bytes 56 | tf_op jit(solution)/shard_map/ppermute | solution.py:12
  14.6 47.0 %collective-permute-start.2 = (s32[4]{0:T(128)S(1)}, s32[4]{0:T(128)S(1)}, u32[]{:S(2)}, u32[]{:S(2)}) collective-permute-start(s32[4]{0:T(128)S(1)} %get-tuple-element.26), channel_id=1, source_target_pairs={{0,4},{4,8},{8,12},{12,16},{16,20},{20,24},{24,28},{28,32},{32,36}... | collective-permute-start | bytes 56 | tf_op jit(solution)/shard_map/ppermute | solution.py:12
  17.1 43.8 %collective-permute-start.1 = (s32[4]{0:T(128)S(1)}, s32[4]{0:T(128)S(1)}, u32[]{:S(2)}, u32[]{:S(2)}) collective-permute-start(s32[4]{0:T(128)S(1)} %get-tuple-element.28), channel_id=1, source_target_pairs={{0,252},{4,0},{8,4},{12,8},{16,12},{20,16},{24,20},{28,24},{32,28}... | collective-permute-start | bytes 56 | tf_op jit(solution)/shard_map/ppermute | solution.py:12
  17.1 43.8 %collective-permute-start = (s32[4]{0:T(128)S(1)}, s32[4]{0:T(128)S(1)}, u32[]{:S(2)}, u32[]{:S(2)}) collective-permute-start(s32[4]{0:T(128)S(1)} %get-tuple-element.29), channel_id=1, source_target_pairs={{0,248},{4,252},{8,0},{12,4},{16,8},{20,12},{24,16},{28,20},{32,24... | collective-permute-start | bytes 56 | tf_op jit(solution)/shard_map/ppermute | solution.py:12
  33.8 13.8 %copy-start = (bf16[2,13,128,128]{3,2,1,0:T(8,128)(2,1)S(1)}, bf16[2,13,128,128]{3,2,1,0:T(8,128)(2,1)}, u32[]{:S(2)}) copy-start(bf16[2,13,128,128]{3,2,1,0:T(8,128)(2,1)} %param.10) | copy-start | bytes 2555908
  53.3 6.8 %copy-start.1 = (s32[2,4]{1,0:T(2,128)S(1)}, s32[2,4]{1,0:T(2,128)}, u32[]{:S(2)}) copy-start(s32[2,4]{1,0:T(2,128)} %param.12) | copy-start | bytes 100
  60.1 56.8 %reduce-scatter.5.cloned.1.call-start = ((), (), s32[]{:S(2)}) async-start(), calls=%async_computation.3 | async-start | bytes 163840 | tf_op jit(solution)/shard_map/reduce_scatter | solution.py:85
  61.5 9.1 %collective-permute-start.8 = (bf16[4,128,128]{2,1,0:T(8,128)(2,1)S(1)}, bf16[4,128,128]{2,1,0:T(8,128)(2,1)S(1)}, u32[]{:S(2)}, u32[]{:S(2)}) collective-permute-start(bf16[4,128,128]{2,1,0:T(8,128)(2,1)S(1)} %gather_fusion.1), channel_id=1, source_target_pairs={{0,8},{4,12},{8,16},{12,20},{16,24},{20,28},{24,32},{28,36},{32,40... | collective-permute-start | bytes 393224 | tf_op jit(solution)/shard_map/ppermute | solution.py:12
  63.5 9.1 %collective-permute-start.10 = (bf16[4,128,128]{2,1,0:T(8,128)(2,1)S(1)}, bf16[4,128,128]{2,1,0:T(8,128)(2,1)S(1)}, u32[]{:S(2)}, u32[]{:S(2)}) collective-permute-start(bf16[4,128,128]{2,1,0:T(8,128)(2,1)S(1)} %gather_fusion.4), channel_id=1, source_target_pairs={{0,252},{4,0},{8,4},{12,8},{16,12},{20,16},{24,20},{28,24},{32,28}... | collective-permute-start | bytes 393224 | tf_op jit(solution)/shard_map/ppermute | solution.py:12
  65.5 7.9 %collective-permute-start.11 = (bf16[4,128,128]{2,1,0:T(8,128)(2,1)S(1)}, bf16[4,128,128]{2,1,0:T(8,128)(2,1)S(1)}, u32[]{:S(2)}, u32[]{:S(2)}) collective-permute-start(bf16[4,128,128]{2,1,0:T(8,128)(2,1)S(1)} %gather_fusion.5), channel_id=1, source_target_pairs={{0,248},{4,252},{8,0},{12,4},{16,8},{20,12},{24,16},{28,20},{32,24... | collective-permute-start | bytes 393224 | tf_op jit(solution)/shard_map/ppermute | solution.py:12
  70.5 2.0 %collective-permute-start.9 = (bf16[4,128,128]{2,1,0:T(8,128)(2,1)S(1)}, bf16[4,128,128]{2,1,0:T(8,128)(2,1)S(1)}, u32[]{:S(2)}, u32[]{:S(2)}) collective-permute-start(bf16[4,128,128]{2,1,0:T(8,128)(2,1)S(1)} %gather_fusion.2), channel_id=1, source_target_pairs={{0,4},{4,8},{8,12},{12,16},{16,20},{20,24},{24,28},{28,32},{32,36}... | collective-permute-start | bytes 393224 | tf_op jit(solution)/shard_map/ppermute | solution.py:12
  82.9 19.2 %collective-permute-start.4 = (f32[4,32,128]{2,0,1:T(4,128)S(1)}, f32[4,32,128]{2,0,1:T(4,128)S(1)}, u32[]{:S(2)}, u32[]{:S(2)}) collective-permute-start(f32[4,32,128]{2,0,1:T(4,128)S(1)} %get-tuple-element.21), channel_id=1, source_target_pairs={{0,248},{4,252},{8,0},{12,4},{16,8},{20,12},{24,16},{28,20},{32,24... | collective-permute-start | bytes 196616 | tf_op jit(solution)/shard_map/ppermute | solution.py:12
  99.3 6.5 %collective-permute-start.7 = (f32[4,32,128]{2,0,1:T(4,128)S(1)}, f32[4,32,128]{2,0,1:T(4,128)S(1)}, u32[]{:S(2)}, u32[]{:S(2)}) collective-permute-start(f32[4,32,128]{2,0,1:T(4,128)S(1)} %get-tuple-element.18), channel_id=1, source_target_pairs={{0,8},{4,12},{8,16},{12,20},{16,24},{20,28},{24,32},{28,36},{32,40... | collective-permute-start | bytes 196616 | tf_op jit(solution)/shard_map/ppermute | solution.py:12
  99.4 4.0 %collective-permute-start.6 = (f32[4,32,128]{2,0,1:T(4,128)S(1)}, f32[4,32,128]{2,0,1:T(4,128)S(1)}, u32[]{:S(2)}, u32[]{:S(2)}) collective-permute-start(f32[4,32,128]{2,0,1:T(4,128)S(1)} %get-tuple-element.19), channel_id=1, source_target_pairs={{0,4},{4,8},{8,12},{12,16},{16,20},{20,24},{24,28},{28,32},{32,36}... | collective-permute-start | bytes 196616 | tf_op jit(solution)/shard_map/ppermute | solution.py:12
  99.6 3.7 %collective-permute-start.5 = (f32[4,32,128]{2,0,1:T(4,128)S(1)}, f32[4,32,128]{2,0,1:T(4,128)S(1)}, u32[]{:S(2)}, u32[]{:S(2)}) collective-permute-start(f32[4,32,128]{2,0,1:T(4,128)S(1)} %get-tuple-element.20), channel_id=1, source_target_pairs={{0,252},{4,0},{8,4},{12,8},{16,12},{20,16},{24,20},{28,24},{32,28}... | collective-permute-start | bytes 196616 | tf_op jit(solution)/shard_map/ppermute | solution.py:12
Sparse Core Ops, SparseCore 0:
  60.2 21.3 reduce-scatter.2
  99.4 17.4 reduce-scatter.4
where the time goes:
time: 128 us; the launch traced here: 126 us
  local copies, waits for them, and re-layouts  35.5 us (28%)
  starting transfers between devices  25.3 us (20%)
  waiting for transfers between devices  24.4 us (19%)
  matrix products  23.3 us (18%)
  between operations  13.7 us (11%)
  other arithmetic  3.4 us (3%)
    ppermute x12, starting transfers between devices, passed_along(): return lax.ppermute(value, axis, pairs)  25.2 us
    gather x2, local copies, waits for them, and re-layouts, local(): paired = jnp.take(blocks, paired_index, axis=0)  23.4 us
    reduce_scatter x1, waiting for transfers between devices, local(): lax.psum_scatter(diagonal, 'aux', scatter_dimension=1, tiled=True)  10.5 us
    dot_general x1, matrix products, local(): jnp.einsum('jpma,jpan->jmn', blocks, left, preferred_element_type=jnp.flo...  10 us
    reduce_scatter x1, waiting for transfers between devices, local(): lax.psum_scatter(cross, 'aux', scatter_dimension=1, tiled=True)  7.57 us
    ppermute x12, waiting for transfers between devices, passed_along(): return lax.ppermute(value, axis, pairs)  6.32 us
    dot_general x1, matrix products, local(): jnp.einsum('jpmn,jpmc->jnc', blocks, right, preferred_element_type=jnp.fl...  5.71 us
    dot_general x1, matrix products, local(): jnp.einsum('gml,gjplc->gjpmc', home_blocks, paired_grouped, preferred_ele...  5.67 us
  transfers between devices with their start and end apart: 14, of which 6 were waited for; matrix products, arithmetic and copies ran while one was open for 43% of the time, Pallas kernels for 0%

commit v1 on v0

v1 whole, which is shorter than its diff:
```python
import jax
import jax.numpy as jnp
from jax import lax
from jax.experimental import pallas as pl
from jax.experimental.pallas import tpu as pltpu
from jax.sharding import PartitionSpec as P

BASIS = 128
SLAB = 8
ROWS = 32
EDGE = 16
f32 = jnp.float32
bf16 = jnp.bfloat16
VM = pl.BlockSpec(memory_space=pltpu.VMEM)
SM = pl.BlockSpec(memory_space=pltpu.SMEM)
ANY = pl.BlockSpec(memory_space=pl.ANY)


def swapped(value, kind):
    count = lax.axis_size("sfc")
    if kind == "a":
        step, first = 1, [0]
        period = 2
    elif kind == "b":
        step, first = 1, [1]
        period = 2
    elif kind == "c":
        step, first = 2, [0, 1]
        period = 4
    else:
        step, first = 2, [2, 3]
        period = 4
    pairs = []
    for base in range(0, count, period):
        for start in first:
            low = (base + start) % count
            high = (base + start + step) % count
            pairs += [(low, high), (high, low)]
    return lax.ppermute(value, "sfc", pairs)


def side_by_side(parts):
    return jnp.concatenate(parts, axis=1)


def stacked(wide, parts):
    return jnp.concatenate([wide[:, BASIS * i : BASIS * (i + 1)] for i in range(parts)], axis=0)


def right_cross(home, paired, block, held):
    aux = paired.shape[0]
    for p in range(0, aux, SLAB):
        wide = side_by_side([paired[p + i] for i in range(SLAB)])
        right = jnp.dot(home, wide, preferred_element_type=f32).astype(bf16)
        held[pl.ds(p * BASIS, SLAB * BASIS)] = stacked(right, SLAB)
    flat = block[...].reshape(aux * BASIS, BASIS)
    return lax.dot_general(flat, held[...], (((0,), (0,)), ((), ())), preferred_element_type=f32)


def left_own(far, paired, block, held):
    aux = paired.shape[0]
    for p in range(0, aux, SLAB):
        tall = paired[pl.ds(p, SLAB)].reshape(SLAB * BASIS, BASIS)
        left = lax.dot_general(
            far, tall, (((1,), (1,)), ((), ())), preferred_element_type=f32
        ).astype(bf16)
        held[pl.ds(p * BASIS, SLAB * BASIS)] = stacked(left, SLAB)
    wide = side_by_side([block[p] for p in range(aux)])
    return jnp.dot(wide, held[...], preferred_element_type=f32)


def geometry(near, pick, mask, mine, total, g, j):
    k = pick[g, j]
    shift = lax.rem(near[g, j] - 2 * mine - g + total + 64, total) - 64
    offset = lax.rem(near[g, k] - near[g, j] + 6 + total, total)
    active = mask[g, j] * mask[g, k]
    return k, shift, offset, active


def pack_kernel(where, density, out_a, out_b, out_c, out_d, sems):
    mine = where[0]
    plus_a = 1 - lax.rem(mine, 2)
    plus_c = 1 - lax.rem(mine, 4) // 2
    copies = []
    for ref, plus in ((out_b, 1 - plus_a), (out_a, plus_a)):
        copies.append((density.at[0, pl.ds(1 + 4 * plus, 8)], ref.at[pl.ds(0, 8)]))
        copies.append((density.at[1, pl.ds(4 * plus, 8)], ref.at[pl.ds(8, 8)]))
    for ref, plus in ((out_d, 1 - plus_c), (out_c, plus_c)):
        copies.append((density.at[plus, pl.ds(6 * plus, 7)], ref))
    made = [pltpu.make_async_copy(s, d, sems.at[i]) for i, (s, d) in enumerate(copies)]
    for copy in made:
        copy.start()
    for copy in made:
        copy.wait()


def cross_kernel(
    where, near, pick, mask, blocks, density, out_a, out_b, out_c, out_d, out_l, own, held
):
    mine = where[0]
    total = where[1]
    odd = lax.rem(mine, 2)
    upper = lax.rem(mine, 4) // 2
    for ref in (out_a, out_b, out_c, out_d, out_l):
        ref[...] = jnp.zeros_like(ref)
    own[...] = jnp.zeros_like(own)

    def visit(i, carry):
        g = i // 4
        j = lax.rem(i, 4)
        k, shift, offset, active = geometry(near, pick, mask, mine, total, g, j)
        place = g + shift
        reach = (place + 4) // 2 - 2
        within = place - 2 * reach
        label = (within * 13 + offset).astype(f32)

        @pl.when(active != 0)
        def _():
            value = right_cross(density[g, 6], blocks.at[g, k], blocks.at[g, j], held)
            value = value.astype(bf16)
            tag = jnp.full((EDGE, BASIS), label, f32).astype(bf16)

            def put(ref, slot):
                ref[slot, pl.ds(0, BASIS)] = value
                ref[slot, pl.ds(BASIS, EDGE)] = tag

            ahead = jnp.where(reach > 0, 1, 0)
            slot = jnp.where(reach > 0, 3 * g + shift - 2, g - shift - 1)
            slot = jnp.clip(slot, 0, 3)
            one = jnp.abs(reach) == 1
            two = jnp.abs(reach) == 2

            @pl.when(reach == 0)
            def _():
                put(out_l, jnp.clip(3 * g + shift, 0, 3))

            @pl.when(jnp.logical_and(one, ahead != odd))
            def _():
                put(out_a, slot)

            @pl.when(jnp.logical_and(one, ahead == odd))
            def _():
                put(out_b, slot)

            @pl.when(jnp.logical_and(two, ahead != upper))
            def _():
                put(out_c, 0)

            @pl.when(jnp.logical_and(two, ahead == upper))
            def _():
                put(out_d, 0)

        @pl.when(jnp.logical_and(active != 0, reach == 0))
        def _():
            far = density[within, offset]
            own[g] += left_own(far, blocks.at[g, k], blocks.at[g, j], held)

        return carry

    lax.fori_loop(0, 8, visit, 0)


def own_kernel(
    where, near, pick, mask, blocks, far_a, far_b, far_c, far_d, own_in, own, held, far
):
    mine = where[0]
    total = where[1]
    odd = lax.rem(mine, 2)
    upper = lax.rem(mine, 4) // 2
    own[...] = own_in[...]

    def visit(i, carry):
        g = i // 4
        j = lax.rem(i, 4)
        k, shift, offset, active = geometry(near, pick, mask, mine, total, g, j)
        place = g + shift
        reach = (place + 4) // 2 - 2
        within = place - 2 * reach
        ahead = jnp.where(reach > 0, 1, 0)

        @pl.when(jnp.logical_and(active != 0, reach != 0))
        def _():
            start = jnp.where(reach > 0, 1 - within, 5 - within)
            index = jnp.clip(within * 8 + offset - start, 0, 15)
            single = jnp.clip(offset - 6 * (1 - ahead), 0, 6)
            one = jnp.abs(reach) == 1
            two = jnp.abs(reach) == 2

            @pl.when(jnp.logical_and(one, ahead != odd))
            def _():
                far[...] = far_a[index]

            @pl.when(jnp.logical_and(one, ahead == odd))
            def _():
                far[...] = far_b[index]

            @pl.when(jnp.logical_and(two, ahead != upper))
            def _():
                far[...] = far_c[single]

            @pl.when(jnp.logical_and(two, ahead == upper))
            def _():
                far[...] = far_d[single]

            own[g] += left_own(far[...], blocks.at[g, k], blocks.at[g, j], held)

        return carry

    lax.fori_loop(0, 8, visit, 0)


def rows_kernel(where, in_a, in_b, in_c, in_d, in_l, own, *outs):
    side = where[2]
    for step, out in enumerate(outs):
        start = pl.multiple_of(lax.rem(side + step + 1, 4) * ROWS, ROWS)
        at = 0
        for ref in (in_a, in_b, in_c, in_d, in_l):
            for slot in range(ref.shape[0]):
                out[at] = ref[slot, pl.ds(start, ROWS)]
                at += 1
        for g in range(2):
            out[at] = own[g, pl.ds(start, ROWS)].astype(bf16)
            at += 1


def band_kernel(where, in_a, in_b, in_c, in_d, in_l, own, from_1, from_2, from_3, band):
    side = where[2]
    start = pl.multiple_of(side * ROWS, ROWS)
    band[...] = jnp.zeros_like(band)

    def others(at):
        return (
            from_1[at].astype(f32) + from_2[at].astype(f32) + from_3[at].astype(f32)
        )

    at = 0
    found = []
    for ref in (in_a, in_b, in_c, in_d, in_l):
        for slot in range(ref.shape[0]):
            label = jnp.max(ref[slot, pl.ds(BASIS, EDGE)].astype(f32)).astype(jnp.int32)
            value = ref[slot, pl.ds(start, ROWS)].astype(f32) + others(at)
            found.append((jnp.clip(label, 0, 25), value))
            at += 1
    for g in range(2):
        found.append((13 * g + 6, own[g, pl.ds(start, ROWS)] + others(at)))
        at += 1
    for label, value in found:
        band[label] += value


def local(three_index, density, neighbours, partner, block_mask):
    total = 2 * lax.axis_size("sfc")
    where = jnp.stack(
        [lax.axis_index("sfc"), jnp.int32(total), lax.axis_index("aux")]
    ).astype(jnp.int32)
    ints = (where, neighbours, partner, block_mask)
    limit = pltpu.CompilerParams(vmem_limit_bytes=24 << 20)

    def shape(*dims, dtype=bf16):
        return jax.ShapeDtypeStruct(dims, dtype)

    packed = pl.pallas_call(
        pack_kernel,
        in_specs=[SM, ANY],
        out_specs=[ANY] * 4,
        out_shape=[shape(16, 128, 128), shape(16, 128, 128), shape(7, 128, 128), shape(7, 128, 128)],
        scratch_shapes=[pltpu.SemaphoreType.DMA((6,))],
        name="pack",
    )(where, density)
    far_b = swapped(packed[1], "b")
    far_d = swapped(packed[3], "d")
    far_a = swapped(packed[0], "a")
    far_c = swapped(packed[2], "c")

    tall = BASIS + EDGE
    crosses = pl.pallas_call(
        cross_kernel,
        in_specs=[SM] * 4 + [VM, VM],
        out_specs=[VM] * 6,
        out_shape=[
            shape(4, tall, 128),
            shape(4, tall, 128),
            shape(1, tall, 128),
            shape(1, tall, 128),
            shape(4, tall, 128),
            shape(2, 128, 128, dtype=f32),
        ],
        scratch_shapes=[pltpu.VMEM((40 * BASIS, BASIS), bf16)],
        compiler_params=limit,
        name="cross",
    )(*ints, three_index, density)
    out_a, out_b, out_c, out_d, in_l, own_near = crosses
    in_b = swapped(out_b, "b")
    in_d = swapped(out_d, "d")
    in_a = swapped(out_a, "a")
    in_c = swapped(out_c, "c")

    own = pl.pallas_call(
        own_kernel,
        in_specs=[SM] * 4 + [VM] * 6,
        out_specs=VM,
        out_shape=shape(2, 128, 128, dtype=f32),
        scratch_shapes=[pltpu.VMEM((40 * BASIS, BASIS), bf16), pltpu.VMEM((128, 128), bf16)],
        compiler_params=limit,
        name="own",
    )(*ints, three_index, far_a, far_b, far_c, far_d, own_near)

    arrived = (in_a, in_b, in_c, in_d, in_l, own)
    sends = pl.pallas_call(
        rows_kernel,
        in_specs=[SM] + [VM] * 6,
        out_specs=[VM] * 3,
        out_shape=[shape(16, ROWS, 128)] * 3,
        name="rows",
    )(where, *arrived)
    received = []
    for step, send in enumerate(sends):
        pairs = [(x, (x + step + 1) % 4) for x in range(4)]
        received.append(lax.ppermute(send, "aux", pairs))
    band = pl.pallas_call(
        band_kernel,
        in_specs=[SM] + [VM] * 9,
        out_specs=VM,
        out_shape=shape(26, ROWS, 128, dtype=f32),
        name="band",
    )(where, *arrived, *received)
    return band.reshape(2, 13, ROWS, 128)


def solution(mesh):
    return jax.shard_map(
        local,
        mesh=mesh,
        in_specs=(
            P("sfc", None, "aux", None, None),
            P("sfc", None, None, None),
            P("sfc", None),
            P("sfc", None),
            P("sfc", None),
        ),
        out_specs=P("sfc", None, "aux", None),
        check_vma=False,
    )
```

time: 128 us -> 103 us (0.80)
  Pallas kernels: 0 us -> 60.6 us
  local copies, waits for them, and re-layouts: 35.5 us -> 11.1 us
  matrix products: 23.3 us -> 0 us
  waiting for transfers between devices: 24.4 us -> 7.05 us
  between operations: 13.7 us -> 0.1 us
  starting transfers between devices: 25.3 us -> 21.6 us
  other arithmetic: 3.4 us -> 0.65 us
    pallas_call x0 -> x5, Pallas kernels: none -> 60.6 us  [the longest x1 47.5 us: local(): pl.pallas_call(pack_kernel, in_specs=[SM, ANY], out_specs=[ANY] * 4, out_...]
    gather x13 -> x0, local copies, waits for them, and re-layouts: 29.8 us -> none  [the longest x2 23.4 us: local(): paired = jnp.take(blocks, paired_index, axis=0)]
    dot_general x5 -> x0, matrix products: 23.3 us -> none  [the longest x1 10 us: local(): jnp.einsum('jpma,jpan->jmn', blocks, left, preferred_element_type=jnp.flo...]
    reduce_scatter x2 -> x0, waiting for transfers between devices: 18 us -> none  [the longest x1 10.5 us: local(): lax.psum_scatter(diagonal, 'aux', scatter_dimension=1, tiled=True)]
    unnamed x12 -> x30, local copies, waits for them, and re-layouts: 0.13 us -> 11.1 us
    ppermute x12 -> x11, starting transfers between devices: 25.2 us -> 21.6 us  [the longest x8 16.8 us: swapped(): return lax.ppermute(value, 'sfc', pairs)]
    reshape x5 -> x0, local copies, waits for them, and re-layouts: 2.44 us -> none  [the longest x2 1.52 us: local(): target = neighbours.reshape(count)]
    ppermute x12 -> x11, waiting for transfers between devices: 6.32 us -> 7.05 us  [the longest x3 4.28 us: local(): received.append(lax.ppermute(send, 'aux', pairs))]
  transfers between devices with their start and end apart: 14 -> 11, of which waited for: 6 -> 3; matrix products, arithmetic and copies ran while one was open for 43% -> 0% of each run, Pallas kernels for 0% -> 9%
where the time goes in v1:
time: 103 us; the launch traced here: 101 us
  Pallas kernels  60.6 us (59%)
  starting transfers between devices  21.6 us (21%)
  local copies, waits for them, and re-layouts  11.1 us (11%)
  waiting for transfers between devices  7.05 us (7%)
    pallas_call x1, Pallas kernels, local(): pl.pallas_call(pack_kernel, in_specs=[SM, ANY], out_specs=[ANY] * 4, out_...  47.5 us
    ppermute x8, starting transfers between devices, swapped(): return lax.ppermute(value, 'sfc', pairs)  16.8 us
    unnamed x30, local copies, waits for them, and re-layouts  11.1 us
    pallas_call x1, Pallas kernels, local(): pl.pallas_call(cross_kernel, in_specs=[SM] * 4 + [VM, VM], out_specs=[VM]...  6.16 us
    ppermute x3, starting transfers between devices, local(): received.append(lax.ppermute(send, 'aux', pairs))  4.81 us
    ppermute x3, waiting for transfers between devices, local(): received.append(lax.ppermute(send, 'aux', pairs))  4.28 us
    ppermute x8, waiting for transfers between devices, swapped(): return lax.ppermute(value, 'sfc', pairs)  2.77 us
    pallas_call x1, Pallas kernels, local(): pl.pallas_call(own_kernel, in_specs=[SM] * 4 + [VM] * 6, out_specs=VM, ou...  2.7 us
  transfers between devices with their start and end apart: 11, of which 3 were waited for; matrix products, arithmetic and copies ran while one was open for 0% of the time, Pallas kernels for 9%

profile of v1, /device:TPU:1, one launch (start us, length us, event | category | flops | bytes accessed | tf_op | source)
XLA Modules:
  0.0 101.1 jit_solution(16469090439716447663)
XLA Ops:
  0.0 0.7 pad_add_fusion.where
  0.7 47.5 %pack.1 = (bf16[16,128,128]{2,1,0:T(8,128)(2,1)}, bf16[16,128,128]{2,1,0:T(8,128)(2,1)}, bf16[7,128,128]{2,1,0:T(8,128)(2,1)}, bf16[7,128,128]{2,1,0:T(8,128)(2,1)}) custom-call(s32[3]{0:T(128)} %pad_add_fusion.where, bf16[2,13,128,128]{3,2,1,0:T(8,128)(2,1)} %density.3), custom_call_target="tpu_custom_call" | custom-call | tf_op jit(solution)/shard_map/pack/pallas_call | solution.py:262
  48.1 3.3 %collective-permute-start.4 = (bf16[16,128,128]{2,1,0:T(8,128)(2,1)}, bf16[16,128,128]{2,1,0:T(8,128)(2,1)S(1)}, u32[]{:S(2)}, u32[]{:S(2)}) collective-permute-start(bf16[16,128,128]{2,1,0:T(8,128)(2,1)} %get-tuple-element.23), channel_id=1, source_target_pairs={{0,4},{4,0},{8,12},{12,8},{16,20},{20,16},{24,28},{28,24},{32,36},... | collective-permute-start | bytes 1572872 | tf_op jit(solution)/shard_map/ppermute | solution.py:39
  51.5 0.0 collective-permute-start.5
  51.5 1.5 %collective-permute-start.6 = (bf16[7,128,128]{2,1,0:T(8,128)(2,1)}, bf16[7,128,128]{2,1,0:T(8,128)(2,1)S(1)}, u32[]{:S(2)}, u32[]{:S(2)}) collective-permute-start(bf16[7,128,128]{2,1,0:T(8,128)(2,1)} %get-tuple-element.25), channel_id=1, source_target_pairs={{0,8},{8,0},{4,12},{12,4},{16,24},{24,16},{20,28},{28,20},{32,40},... | collective-permute-start | bytes 688136 | tf_op jit(solution)/shard_map/ppermute | solution.py:39
  53.0 6.2 %collective-permute-start.7 = (bf16[7,128,128]{2,1,0:T(8,128)(2,1)}, bf16[7,128,128]{2,1,0:T(8,128)(2,1)S(1)}, u32[]{:S(2)}, u32[]{:S(2)}) collective-permute-start(bf16[7,128,128]{2,1,0:T(8,128)(2,1)} %get-tuple-element.26), channel_id=1, source_target_pairs={{8,16},{16,8},{12,20},{20,12},{24,32},{32,24},{28,36},{36,28},{40,... | collective-permute-start | bytes 688136 | tf_op jit(solution)/shard_map/ppermute | solution.py:39
  59.2 0.0 copy-start
  59.2 4.0 %copy-done = bf16[2,4,40,128,128]{4,3,2,1,0:T(8,128)(2,1)S(1)} copy-done((bf16[2,4,40,128,128]{4,3,2,1,0:T(8,128)(2,1)S(1)}, bf16[2,4,40,128,128]{4,3,2,1,0:T(8,128)(2,1)}, u32[]{:S(2)}) %copy-start) | copy-done | bytes 10485784
  63.2 0.0 copy-start.1
  63.2 1.2 %copy-done.1 = bf16[2,13,128,128]{3,2,1,0:T(8,128)(2,1)S(1)} copy-done((bf16[2,13,128,128]{3,2,1,0:T(8,128)(2,1)S(1)}, bf16[2,13,128,128]{3,2,1,0:T(8,128)(2,1)}, u32[]{:S(2)}) %copy-start.1) | copy-done | bytes 851992
  64.4 0.7 copy-done.4
  65.0 0.7 copy-done.5
  65.7 0.7 copy-done.6
  66.4 0.7 copy-done.7
  67.1 6.2 %cross.1 = (bf16[4,144,128]{2,1,0:T(8,128)(2,1)S(1)}, bf16[4,144,128]{2,1,0:T(8,128)(2,1)S(1)}, bf16[1,144,128]{2,1,0:T(8,128)(2,1)S(1)}, bf16[1,144,128]{2,1,0:...) custom-call(s32[3]{0:T(128)S(1)} %copy-done.4, s32[2,4]{1,0:T(2,128)S(1)} %copy-done.5, ...), custom_call_target="tpu_custom_call" | custom-call | tf_op jit(solution)/shard_map/cross/pallas_call | solution.py:276
  73.2 0.0 copy-start.3
  73.2 0.7 copy-done.3
  73.9 0.0 collective-permute-start
  73.9 0.0 collective-permute-done.6.far_c
  73.9 0.0 collective-permute-start.1
  73.9 0.0 collective-permute-done.7.far_d
  73.9 5.7 %collective-permute-start.2 = (bf16[1,144,128]{2,1,0:T(8,128)(2,1)S(1)}, bf16[1,144,128]{2,1,0:T(8,128)(2,1)S(1)}, u32[]{:S(2)}, u32[]{:S(2)}) collective-permute-start(bf16[1,144,128]{2,1,0:T(8,128)(2,1)S(1)} %get-tuple-element.20), channel_id=1, source_target_pairs={{0,8},{8,0},{4,12},{12,4},{16,24},{24,16},{20,28},{28,20},{32,40},... | collective-permute-start | bytes 110600 | tf_op jit(solution)/shard_map/ppermute | solution.py:39
  79.7 0.0 collective-permute-done.4.far_a
  79.7 0.0 collective-permute-start.3
  79.7 0.0 collective-permute-done.5.far_b
  79.7 2.7 %own.1 = f32[2,128,128]{2,1,0:T(8,128)S(1)} custom-call(s32[3]{0:T(128)S(1)} %copy-done.4, s32[2,4]{1,0:T(2,128)S(1)} %copy-done.5, s32[2,4]{1,0:T(2,128)S(1)} %copy-done.6, s32[2,4]{1,0:T(2,128)S(1)} %copy-done.7, bf16[2,4,40,128,128]{4,3,2,1,0:T(8,128)(2,1)S(1)} %copy-done, bf16[16,128,128]{2,1,0:T(8,128)(2,1)S(1)} %collective-permute-done.4.far_a, ...), custom_call_target="tpu_custom_call" | custom-call | tf_op jit(solution)/shard_map/own/pallas_call | solution.py:298
  82.4 0.0 copy-start.2
  82.4 0.6 copy-done.2
  83.0 0.0 collective-permute-done.2.in_c
  83.0 2.8 %collective-permute-done.3.in_d = bf16[1,144,128]{2,1,0:T(8,128)(2,1)S(1)} collective-permute-done((bf16[1,144,128]{2,1,0:T(8,128)(2,1)S(1)}, bf16[1,144,128]{2,1,0:T(8,128)(2,1)S(1)}, u32[]{:S(2)}, u32[]{:S(2)}) %collective-permute-start.3) | collective-permute-done | bytes 36896 | tf_op jit(solution)/shard_map/ppermute | solution.py:39
  85.8 0.0 collective-permute-done.in_a
  85.8 0.0 collective-permute-done.1.in_b
  85.8 0.0 copy-start.9
  85.8 0.0 copy-done.10
  85.8 0.6 copy-done.11
  86.4 0.1 copy-done.8
  86.5 0.1 copy-done.9
  86.5 1.9 %rows.1 = (bf16[16,32,128]{2,1,0:T(8,128)(2,1)}, bf16[16,32,128]{2,1,0:T(8,128)(2,1)}, bf16[16,32,128]{2,1,0:T(8,128)(2,1)}) custom-call(s32[3]{0:T(128)} %pad_add_fusion.where, bf16[4,144,128]{2,1,0:T(8,128)(2,1)} %copy-done.8, bf16[4,144,128]{2,1,0:T(8,128)(2,1)} %copy-done.9, bf16[1,144,128]{2,1,0:T(8,128)(2,1)} %copy-done.10, ...), custom_call_target="tpu_custom_call" | custom-call | tf_op jit(solution)/shard_map/rows/pallas_call | solution.py:309
  88.5 1.2 %collective-permute-start.8 = (bf16[16,32,128]{2,1,0:T(8,128)(2,1)}, bf16[16,32,128]{2,1,0:T(8,128)(2,1)S(1)}, u32[]{:S(2)}, u32[]{:S(2)}) collective-permute-start(bf16[16,32,128]{2,1,0:T(8,128)(2,1)} %get-tuple-element.28), channel_id=1, source_target_pairs={{0,1},{1,2},{2,3},{3,0},{4,5},{5,6},{6,7},{7,4},{8,9},{9,10},{10,1... | collective-permute-start | bytes 393224 | tf_op jit(solution)/shard_map/ppermute | solution.py:319
  89.7 2.4 %collective-permute-start.9 = (bf16[16,32,128]{2,1,0:T(8,128)(2,1)}, bf16[16,32,128]{2,1,0:T(8,128)(2,1)S(1)}, u32[]{:S(2)}, u32[]{:S(2)}) collective-permute-start(bf16[16,32,128]{2,1,0:T(8,128)(2,1)} %get-tuple-element.29), channel_id=1, source_target_pairs={{0,2},{1,3},{2,0},{3,1},{4,6},{5,7},{6,4},{7,5},{8,10},{9,11},{10,... | collective-permute-start | bytes 393224 | tf_op jit(solution)/shard_map/ppermute | solution.py:319
  92.1 1.2 %collective-permute-start.10 = (bf16[16,32,128]{2,1,0:T(8,128)(2,1)}, bf16[16,32,128]{2,1,0:T(8,128)(2,1)S(1)}, u32[]{:S(2)}, u32[]{:S(2)}) collective-permute-start(bf16[16,32,128]{2,1,0:T(8,128)(2,1)} %get-tuple-element.30), channel_id=1, source_target_pairs={{0,3},{1,0},{2,1},{3,2},{4,7},{5,4},{6,5},{7,6},{8,11},{9,8},{10,9... | collective-permute-start | bytes 393224 | tf_op jit(solution)/shard_map/ppermute | solution.py:319
  93.3 1.2 %collective-permute-done.8.from_1 = bf16[16,32,128]{2,1,0:T(8,128)(2,1)S(1)} collective-permute-done((bf16[16,32,128]{2,1,0:T(8,128)(2,1)}, bf16[16,32,128]{2,1,0:T(8,128)(2,1)S(1)}, u32[]{:S(2)}, u32[]{:S(2)}) %collective-permute-start.8) | collective-permute-done | bytes 131104 | tf_op jit(solution)/shard_map/ppermute | solution.py:319
  94.5 3.1 %collective-permute-done.9.from_2 = bf16[16,32,128]{2,1,0:T(8,128)(2,1)S(1)} collective-permute-done((bf16[16,32,128]{2,1,0:T(8,128)(2,1)}, bf16[16,32,128]{2,1,0:T(8,128)(2,1)S(1)}, u32[]{:S(2)}, u32[]{:S(2)}) %collective-permute-start.9) | collective-permute-done | bytes 131104 | tf_op jit(solution)/shard_map/ppermute | solution.py:319
  97.6 0.0 collective-permute-done.10.from_3
  97.6 0.0 copy-done.12
  97.6 0.6 copy-done.13
  98.2 0.7 copy-done.14
  98.9 2.3 %band.1 = f32[26,32,128]{2,1,0:T(8,128)} custom-call(s32[3]{0:T(128)} %pad_add_fusion.where, bf16[4,144,128]{2,1,0:T(8,128)(2,1)} %copy-done.8, bf16[4,144,128]{2,1,0:T(8,128)(2,1)} %copy-done.9, bf16[1,144,128]{2,1,0:T(8,128)(2,1)} %copy-done.10, bf16[1,144,128]{2,1,0:T(8,128)(2,1)} %copy-done.11, bf16[4,144,128]{2,1,0:T(8,128)(2,1)} %copy-done.3, ...), custom_call_target="tpu_custom_call" | custom-call | tf_op jit(solution)/shard_map/band/pallas_call | solution.py:320
  (10 shorter events, 0.0 us)
Async XLA Ops:
  48.1 31.5 %collective-permute-start.4 = (bf16[16,128,128]{2,1,0:T(8,128)(2,1)}, bf16[16,128,128]{2,1,0:T(8,128)(2,1)S(1)}, u32[]{:S(2)}, u32[]{:S(2)}) collective-permute-start(bf16[16,128,128]{2,1,0:T(8,128)(2,1)} %get-tuple-element.23), channel_id=1, source_target_pairs={{0,4},{4,0},{8,12},{12,8},{16,20},{20,16},{24,28},{28,24},{32,36},... | collective-permute-start | bytes 1572872 | tf_op jit(solution)/shard_map/ppermute | solution.py:39
  51.5 28.2 %collective-permute-start.5 = (bf16[16,128,128]{2,1,0:T(8,128)(2,1)}, bf16[16,128,128]{2,1,0:T(8,128)(2,1)S(1)}, u32[]{:S(2)}, u32[]{:S(2)}) collective-permute-start(bf16[16,128,128]{2,1,0:T(8,128)(2,1)} %get-tuple-element.24), channel_id=1, source_target_pairs={{4,8},{8,4},{12,16},{16,12},{20,24},{24,20},{28,32},{32,28},{36,40... | collective-permute-start | bytes 1572872 | tf_op jit(solution)/shard_map/ppermute | solution.py:39
  51.5 22.4 %collective-permute-start.6 = (bf16[7,128,128]{2,1,0:T(8,128)(2,1)}, bf16[7,128,128]{2,1,0:T(8,128)(2,1)S(1)}, u32[]{:S(2)}, u32[]{:S(2)}) collective-permute-start(bf16[7,128,128]{2,1,0:T(8,128)(2,1)} %get-tuple-element.25), channel_id=1, source_target_pairs={{0,8},{8,0},{4,12},{12,4},{16,24},{24,16},{20,28},{28,20},{32,40},... | collective-permute-start | bytes 688136 | tf_op jit(solution)/shard_map/ppermute | solution.py:39
  53.0 20.9 %collective-permute-start.7 = (bf16[7,128,128]{2,1,0:T(8,128)(2,1)}, bf16[7,128,128]{2,1,0:T(8,128)(2,1)S(1)}, u32[]{:S(2)}, u32[]{:S(2)}) collective-permute-start(bf16[7,128,128]{2,1,0:T(8,128)(2,1)} %get-tuple-element.26), channel_id=1, source_target_pairs={{8,16},{16,8},{12,20},{20,12},{24,32},{32,24},{28,36},{36,28},{40,... | collective-permute-start | bytes 688136 | tf_op jit(solution)/shard_map/ppermute | solution.py:39
  59.2 4.0 %copy-start = (bf16[2,4,40,128,128]{4,3,2,1,0:T(8,128)(2,1)S(1)}, bf16[2,4,40,128,128]{4,3,2,1,0:T(8,128)(2,1)}, u32[]{:S(2)}) copy-start(bf16[2,4,40,128,128]{4,3,2,1,0:T(8,128)(2,1)} %blocks.3) | copy-start | bytes 31457284
  63.2 1.2 %copy-start.1 = (bf16[2,13,128,128]{3,2,1,0:T(8,128)(2,1)S(1)}, bf16[2,13,128,128]{3,2,1,0:T(8,128)(2,1)}, u32[]{:S(2)}) copy-start(bf16[2,13,128,128]{3,2,1,0:T(8,128)(2,1)} %density.3) | copy-start | bytes 2555908
  64.4 0.7 copy-start.4
  65.0 0.7 copy-start.5
  65.7 0.7 copy-start.6
  66.4 0.7 copy-start.7
  73.2 0.7 copy-start.3
  73.9 11.9 %collective-permute-start = (bf16[4,144,128]{2,1,0:T(8,128)(2,1)S(1)}, bf16[4,144,128]{2,1,0:T(8,128)(2,1)S(1)}, u32[]{:S(2)}, u32[]{:S(2)}) collective-permute-start(bf16[4,144,128]{2,1,0:T(8,128)(2,1)S(1)} %get-tuple-element.18), channel_id=1, source_target_pairs={{0,4},{4,0},{8,12},{12,8},{16,20},{20,16},{24,28},{28,24},{32,36},... | collective-permute-start | bytes 442376 | tf_op jit(solution)/shard_map/ppermute | solution.py:39
  73.9 11.9 %collective-permute-start.1 = (bf16[4,144,128]{2,1,0:T(8,128)(2,1)S(1)}, bf16[4,144,128]{2,1,0:T(8,128)(2,1)S(1)}, u32[]{:S(2)}, u32[]{:S(2)}) collective-permute-start(bf16[4,144,128]{2,1,0:T(8,128)(2,1)S(1)} %get-tuple-element.19), channel_id=1, source_target_pairs={{4,8},{8,4},{12,16},{16,12},{20,24},{24,20},{28,32},{32,28},{36,40... | collective-permute-start | bytes 442376 | tf_op jit(solution)/shard_map/ppermute | solution.py:39
  73.9 9.1 %collective-permute-start.2 = (bf16[1,144,128]{2,1,0:T(8,128)(2,1)S(1)}, bf16[1,144,128]{2,1,0:T(8,128)(2,1)S(1)}, u32[]{:S(2)}, u32[]{:S(2)}) collective-permute-start(bf16[1,144,128]{2,1,0:T(8,128)(2,1)S(1)} %get-tuple-element.20), channel_id=1, source_target_pairs={{0,8},{8,0},{4,12},{12,4},{16,24},{24,16},{20,28},{28,20},{32,40},... | collective-permute-start | bytes 110600 | tf_op jit(solution)/shard_map/ppermute | solution.py:39
  79.7 6.1 %collective-permute-start.3 = (bf16[1,144,128]{2,1,0:T(8,128)(2,1)S(1)}, bf16[1,144,128]{2,1,0:T(8,128)(2,1)S(1)}, u32[]{:S(2)}, u32[]{:S(2)}) collective-permute-start(bf16[1,144,128]{2,1,0:T(8,128)(2,1)S(1)} %get-tuple-element.21), channel_id=1, source_target_pairs={{8,16},{16,8},{12,20},{20,12},{24,32},{32,24},{28,36},{36,28},{40,... | collective-permute-start | bytes 110600 | tf_op jit(solution)/shard_map/ppermute | solution.py:39
  82.4 0.7 copy-start.2
  83.0 2.8 %copy-start.10 = (bf16[1,144,128]{2,1,0:T(8,128)(2,1)}, bf16[1,144,128]{2,1,0:T(8,128)(2,1)S(1)}, u32[]{:S(2)}) copy-start(bf16[1,144,128]{2,1,0:T(8,128)(2,1)S(1)} %collective-permute-done.2.in_c) | copy-start | bytes 110596
  85.8 0.6 copy-start.11
  85.8 0.7 copy-start.8
  85.8 0.7 copy-start.9
  88.5 6.0 %collective-permute-start.8 = (bf16[16,32,128]{2,1,0:T(8,128)(2,1)}, bf16[16,32,128]{2,1,0:T(8,128)(2,1)S(1)}, u32[]{:S(2)}, u32[]{:S(2)}) collective-permute-start(bf16[16,32,128]{2,1,0:T(8,128)(2,1)} %get-tuple-element.28), channel_id=1, source_target_pairs={{0,1},{1,2},{2,3},{3,0},{4,5},{5,6},{6,7},{7,4},{8,9},{9,10},{10,1... | collective-permute-start | bytes 393224 | tf_op jit(solution)/shard_map/ppermute | solution.py:319
  89.7 7.9 %collective-permute-start.9 = (bf16[16,32,128]{2,1,0:T(8,128)(2,1)}, bf16[16,32,128]{2,1,0:T(8,128)(2,1)S(1)}, u32[]{:S(2)}, u32[]{:S(2)}) collective-permute-start(bf16[16,32,128]{2,1,0:T(8,128)(2,1)} %get-tuple-element.29), channel_id=1, source_target_pairs={{0,2},{1,3},{2,0},{3,1},{4,6},{5,7},{6,4},{7,5},{8,10},{9,11},{10,... | collective-permute-start | bytes 393224 | tf_op jit(solution)/shard_map/ppermute | solution.py:319
  92.1 5.4 %collective-permute-start.10 = (bf16[16,32,128]{2,1,0:T(8,128)(2,1)}, bf16[16,32,128]{2,1,0:T(8,128)(2,1)S(1)}, u32[]{:S(2)}, u32[]{:S(2)}) collective-permute-start(bf16[16,32,128]{2,1,0:T(8,128)(2,1)} %get-tuple-element.30), channel_id=1, source_target_pairs={{0,3},{1,0},{2,1},{3,2},{4,7},{5,4},{6,5},{7,6},{8,11},{9,8},{10,9... | collective-permute-start | bytes 393224 | tf_op jit(solution)/shard_map/ppermute | solution.py:319
  94.4 3.1 %copy-start.12 = (bf16[16,32,128]{2,1,0:T(8,128)(2,1)}, bf16[16,32,128]{2,1,0:T(8,128)(2,1)S(1)}, u32[]{:S(2)}) copy-start(bf16[16,32,128]{2,1,0:T(8,128)(2,1)S(1)} %collective-permute-done.8.from_1) | copy-start | bytes 393220
  97.6 0.6 copy-start.13
  98.2 0.7 copy-start.14

commit v2 on v1

v2 whole, which is shorter than its diff:
```python
import jax
import jax.numpy as jnp
from jax import lax
from jax.experimental import pallas as pl
from jax.experimental.pallas import tpu as pltpu
from jax.sharding import PartitionSpec as P

BASIS = 128
SLAB = 8
ROWS = 32
EDGE = 16
f32 = jnp.float32
bf16 = jnp.bfloat16
VM = pl.BlockSpec(memory_space=pltpu.VMEM)
SM = pl.BlockSpec(memory_space=pltpu.SMEM)
ANY = pl.BlockSpec(memory_space=pl.ANY)


def swapped(value, kind):
    count = lax.axis_size("sfc")
    if kind == "a":
        step, first = 1, [0]
        period = 2
    elif kind == "b":
        step, first = 1, [1]
        period = 2
    elif kind == "c":
        step, first = 2, [0, 1]
        period = 4
    else:
        step, first = 2, [2, 3]
        period = 4
    pairs = []
    for base in range(0, count, period):
        for start in first:
            low = (base + start) % count
            high = (base + start + step) % count
            pairs += [(low, high), (high, low)]
    return lax.ppermute(value, "sfc", pairs)


def side_by_side(parts):
    return jnp.concatenate(parts, axis=1)


def stacked(wide, parts):
    return jnp.concatenate([wide[:, BASIS * i : BASIS * (i + 1)] for i in range(parts)], axis=0)


def right_cross(home, paired, block, held):
    aux = paired.shape[0]
    for p in range(0, aux, SLAB):
        wide = side_by_side([paired[p + i] for i in range(SLAB)])
        right = jnp.dot(home, wide, preferred_element_type=f32).astype(bf16)
        held[pl.ds(p * BASIS, SLAB * BASIS)] = stacked(right, SLAB)
    flat = block[...].reshape(aux * BASIS, BASIS)
    return lax.dot_general(flat, held[...], (((0,), (0,)), ((), ())), preferred_element_type=f32)


def left_own(far, paired, block, held):
    aux = paired.shape[0]
    for p in range(0, aux, SLAB):
        tall = paired[pl.ds(p, SLAB)].reshape(SLAB * BASIS, BASIS)
        left = lax.dot_general(
            far, tall, (((1,), (1,)), ((), ())), preferred_element_type=f32
        ).astype(bf16)
        held[pl.ds(p * BASIS, SLAB * BASIS)] = stacked(left, SLAB)
    wide = side_by_side([block[p] for p in range(aux)])
    return jnp.dot(wide, held[...], preferred_element_type=f32)


def fetch_ints(sources, targets, sems):
    copies = [pltpu.make_async_copy(s, t, sems.at[i]) for i, (s, t) in enumerate(zip(sources, targets))]
    for copy in copies:
        copy.start()
    for copy in copies:
        copy.wait()


class Pair:
    def __init__(self, i, near, pick, mask):
        mine = lax.axis_index("sfc")
        total = 2 * lax.axis_size("sfc")
        self.g = g = i // 4
        self.j = j = lax.rem(i, 4)
        self.k = k = pick[g, j]
        self.shift = lax.rem(near[g, j] - 2 * mine - g + total + 64, total) - 64
        self.offset = lax.rem(near[g, k] - near[g, j] + 6 + total, total)
        self.active = mask[g, j] * mask[g, k] != 0
        place = g + self.shift
        self.reach = (place + 4) // 2 - 2
        self.within = place - 2 * self.reach
        self.ahead = jnp.where(self.reach > 0, 1, 0)
        one = jnp.abs(self.reach) == 1
        two = jnp.abs(self.reach) == 2
        odd = lax.rem(mine, 2)
        upper = lax.rem(mine, 4) // 2
        self.in_a = jnp.logical_and(one, self.ahead != odd)
        self.in_b = jnp.logical_and(one, self.ahead == odd)
        self.in_c = jnp.logical_and(two, self.ahead != upper)
        self.in_d = jnp.logical_and(two, self.ahead == upper)
        self.one = one
        self.two = two

    def when(self, condition):
        return pl.when(jnp.logical_and(self.active, condition))


def pack_kernel(density, out_b, out_d, out_a, out_c, sems):
    mine = lax.axis_index("sfc")
    plus_a = 1 - lax.rem(mine, 2)
    plus_c = 1 - lax.rem(mine, 4) // 2
    copies = []
    for ref, plus in ((out_b, 1 - plus_a), (out_a, plus_a)):
        copies.append((density.at[0, pl.ds(1 + 4 * plus, 8)], ref.at[pl.ds(0, 8)]))
        copies.append((density.at[1, pl.ds(4 * plus, 8)], ref.at[pl.ds(8, 8)]))
    for ref, plus in ((out_d, 1 - plus_c), (out_c, plus_c)):
        copies.append((density.at[plus, pl.ds(6 * plus, 7)], ref))
    made = [pltpu.make_async_copy(s, d, sems.at[i]) for i, (s, d) in enumerate(copies)]
    for copy in made:
        copy.start()
    for copy in made:
        copy.wait()


def put(ref, slot, value, pair):
    label = (pair.within * 13 + pair.offset).astype(f32)
    ref[slot, pl.ds(0, BASIS)] = value
    ref[slot, pl.ds(BASIS, EDGE)] = jnp.full((EDGE, BASIS), label, f32).astype(bf16)


def cross_kernel(
    near_in, pick_in, mask_in, source, density,
    out_b, out_d, out_a, out_c, inside, blocks,
    near, pick, mask, home, held, int_sems, home_sem, sems,
):
    def loads(g):
        return [
            pltpu.make_async_copy(source.at[g, j], blocks.at[g, j], sems.at[g, j])
            for j in range(4)
        ]

    center = pltpu.make_async_copy(density.at[:, 6], home, home_sem)
    center.start()
    for copy in loads(0):
        copy.start()
    fetch_ints((near_in, pick_in, mask_in), (near, pick, mask), int_sems)
    for ref in (out_b, out_d, out_a, out_c, inside):
        ref[...] = jnp.zeros_like(ref)
    center.wait()

    def visit(i, carry):
        pair = Pair(i, near, pick, mask)
        g, j, k, shift = pair.g, pair.j, pair.k, pair.shift

        @pl.when(pair.active)
        def _():
            value = right_cross(home[g], blocks.at[g, k], blocks.at[g, j], held).astype(bf16)
            slot = jnp.where(pair.reach > 0, 3 * g + shift - 2, g - shift - 1)
            slot = jnp.clip(slot, 0, 3)

            @pl.when(pair.reach == 0)
            def _():
                put(inside, jnp.clip(3 * g + shift, 0, 3), value, pair)

            @pl.when(pair.in_a)
            def _():
                put(out_a, slot, value, pair)

            @pl.when(pair.in_b)
            def _():
                put(out_b, slot, value, pair)

            @pl.when(pair.in_c)
            def _():
                put(out_c, 0, value, pair)

            @pl.when(pair.in_d)
            def _():
                put(out_d, 0, value, pair)

        return carry

    def group(g, carry):
        for j in range(4):
            pltpu.make_async_copy(source.at[0, 0], blocks.at[0, 0], sems.at[g, j]).wait()

        @pl.when(g == 0)
        def _():
            for copy in loads(1):
                copy.start()

        return lax.fori_loop(4 * g, 4 * g + 4, visit, carry)

    lax.fori_loop(0, 2, group, 0)


def own_kernel(
    far_b, far_d, far_a, far_c, near_in, pick_in, mask_in, blocks, density, own,
    near, pick, mask, held, far, whole, int_sems, whole_sem,
):
    copy = pltpu.make_async_copy(density, whole, whole_sem)
    copy.start()
    fetch_ints((near_in, pick_in, mask_in), (near, pick, mask), int_sems)
    own[...] = jnp.zeros_like(own)
    copy.wait()

    def visit(i, carry):
        pair = Pair(i, near, pick, mask)
        g, j, k = pair.g, pair.j, pair.k

        @pl.when(pair.active)
        def _():
            start = jnp.where(pair.reach > 0, 1 - pair.within, 5 - pair.within)
            index = jnp.clip(pair.within * 8 + pair.offset - start, 0, 15)
            single = jnp.clip(pair.offset - 6 * (1 - pair.ahead), 0, 6)

            @pl.when(pair.reach == 0)
            def _():
                far[...] = whole[pair.within, pair.offset]

            @pl.when(pair.in_a)
            def _():
                far[...] = far_a[index]

            @pl.when(pair.in_b)
            def _():
                far[...] = far_b[index]

            @pl.when(pair.in_c)
            def _():
                far[...] = far_c[single]

            @pl.when(pair.in_d)
            def _():
                far[...] = far_d[single]

            own[g] += left_own(far[...], blocks.at[g, k], blocks.at[g, j], held)

        return carry

    lax.fori_loop(0, 8, visit, 0)


def rows_kernel(in_b, in_d, in_a, in_c, in_l, own, *outs):
    side = lax.axis_index("aux")
    for step, out in enumerate(outs):
        start = pl.multiple_of(lax.rem(side + step + 1, 4) * ROWS, ROWS)
        at = 0
        for ref in (in_b, in_d, in_a, in_c, in_l):
            for slot in range(ref.shape[0]):
                out[at] = ref[slot, pl.ds(start, ROWS)]
                at += 1
        for g in range(2):
            out[at] = own[g, pl.ds(start, ROWS)].astype(bf16)
            at += 1


def band_kernel(in_b, in_d, in_a, in_c, in_l, own, from_1, from_2, from_3, band):
    side = lax.axis_index("aux")
    start = pl.multiple_of(side * ROWS, ROWS)
    band[...] = jnp.zeros_like(band)

    def others(at):
        return (
            from_1[at].astype(f32) + from_2[at].astype(f32) + from_3[at].astype(f32)
        )

    at = 0
    found = []
    for ref in (in_b, in_d, in_a, in_c, in_l):
        for slot in range(ref.shape[0]):
            label = jnp.max(ref[slot, pl.ds(BASIS, EDGE)].astype(f32)).astype(jnp.int32)
            value = ref[slot, pl.ds(start, ROWS)].astype(f32) + others(at)
            found.append((jnp.clip(label, 0, 25), value))
            at += 1
    for g in range(2):
        found.append((13 * g + 6, own[g, pl.ds(start, ROWS)] + others(at)))
        at += 1
    for label, value in found:
        band[label] += value


def shape(*dims, dtype=bf16):
    return jax.ShapeDtypeStruct(dims, dtype)


def int_scratch():
    return [pltpu.SMEM((2, 4), jnp.int32)] * 3


def local(three_index, density, neighbours, partner, block_mask):
    limit = pltpu.CompilerParams(vmem_limit_bytes=8 << 20)
    small = pltpu.CompilerParams(vmem_limit_bytes=4 << 20)
    three_index, density, neighbours, partner, block_mask = [
        pltpu.with_memory_space_constraint(x, pltpu.HBM)
        for x in (three_index, density, neighbours, partner, block_mask)
    ]
    ints = (neighbours, partner, block_mask)
    dma = pltpu.SemaphoreType.DMA
    packed = pl.pallas_call(
        pack_kernel,
        in_specs=[ANY],
        out_specs=[VM] * 4,
        out_shape=[shape(16, 128, 128), shape(7, 128, 128), shape(16, 128, 128), shape(7, 128, 128)],
        scratch_shapes=[dma((6,))],
        compiler_params=small,
        name="pack",
    )(density)
    far_b = swapped(packed[0], "b")
    far_d = swapped(packed[1], "d")
    far_a = swapped(packed[2], "a")
    far_c = swapped(packed[3], "c")

    tall = BASIS + EDGE
    held = pltpu.VMEM((40 * BASIS, BASIS), bf16)
    out_b, out_d, out_a, out_c, inside, blocks = pl.pallas_call(
        cross_kernel,
        in_specs=[ANY] * 5,
        out_specs=[VM] * 6,
        out_shape=[
            shape(4, tall, 128),
            shape(1, tall, 128),
            shape(4, tall, 128),
            shape(1, tall, 128),
            shape(4, tall, 128),
            pltpu.VMEM(three_index.shape, bf16),
        ],
        scratch_shapes=int_scratch()
        + [pltpu.VMEM((2, 128, 128), bf16), held]
        + [dma((3,)), dma(()), dma((2, 4))],
        compiler_params=limit,
        name="cross",
    )(*ints, three_index, density)
    in_b = swapped(out_b, "b")
    in_d = swapped(out_d, "d")
    in_a = swapped(out_a, "a")
    in_c = swapped(out_c, "c")

    own = pl.pallas_call(
        own_kernel,
        in_specs=[VM] * 4 + [ANY] * 3 + [VM, ANY],
        out_specs=VM,
        out_shape=shape(2, 128, 128, dtype=f32),
        scratch_shapes=int_scratch()
        + [held, pltpu.VMEM((128, 128), bf16), pltpu.VMEM(density.shape, bf16), dma((3,)), dma(())],
        compiler_params=limit,
        name="own",
    )(far_b, far_d, far_a, far_c, *ints, blocks, density)

    arrived = (in_b, in_d, in_a, in_c, inside, own)
    sends = pl.pallas_call(
        rows_kernel,
        in_specs=[VM] * 6,
        out_specs=[VM] * 3,
        out_shape=[shape(16, ROWS, 128)] * 3,
        compiler_params=small,
        name="rows",
    )(*arrived)
    received = []
    for step, send in enumerate(sends):
        pairs = [(x, (x + step + 1) % 4) for x in range(4)]
        received.append(lax.ppermute(send, "aux", pairs))
    band = pl.pallas_call(
        band_kernel,
        in_specs=[VM] * 9,
        out_specs=VM,
        out_shape=shape(26, ROWS, 128, dtype=f32),
        compiler_params=small,
        name="band",
    )(*arrived, *received)
    return band.reshape(2, 13, ROWS, 128)


def solution(mesh):
    return jax.shard_map(
        local,
        mesh=mesh,
        in_specs=(
            P("sfc", None, "aux", None, None),
            P("sfc", None, None, None),
            P("sfc", None),
            P("sfc", None),
            P("sfc", None),
        ),
        out_specs=P("sfc", None, "aux", None),
        check_vma=False,
    )
```

time: 103 us -> 45.6 us (0.44); the launches traced: 101 us -> 45.9 us
  Pallas kernels: 60.6 us -> 20.6 us
  local copies, waits for them, and re-layouts: 11.1 us -> 0 us
  waiting for transfers between devices: 7.05 us -> 3.62 us
    pallas_call x5, Pallas kernels: 60.6 us -> 20.6 us  [the longest x1 9.76 us: local(): pl.pallas_call(cross_kernel, in_specs=[ANY] * 5, out_specs=[VM] * 6, out_...]
    unnamed x30 -> x0, local copies, waits for them, and re-layouts: 11.1 us -> none
    ppermute x8, waiting for transfers between devices: 2.77 us -> 0.02 us  [swapped(): return lax.ppermute(value, 'sfc', pairs)]
  transfers between devices with their start and end apart: 11 -> 11, of which waited for: 3 -> 2; matrix products, arithmetic and copies ran while one was open for 0% -> 0% of each run, Pallas kernels for 9% -> 40%
where the time goes in v2:
time: 45.6 us; the launch traced here: 45.9 us
  starting transfers between devices  21.6 us (47%)
  Pallas kernels  20.6 us (45%)
  waiting for transfers between devices  3.62 us (8%)
    ppermute x8, starting transfers between devices, swapped(): return lax.ppermute(value, 'sfc', pairs)  16.7 us
    pallas_call x1, Pallas kernels, local(): pl.pallas_call(cross_kernel, in_specs=[ANY] * 5, out_specs=[VM] * 6, out_...  9.76 us
    pallas_call x1, Pallas kernels, local(): pl.pallas_call(own_kernel, in_specs=[VM] * 4 + [ANY] * 3 + [VM, ANY], out...  8.42 us
    ppermute x3, starting transfers between devices, local(): received.append(lax.ppermute(send, 'aux', pairs))  4.9 us
    ppermute x3, waiting for transfers between devices, local(): received.append(lax.ppermute(send, 'aux', pairs))  3.59 us
    pallas_call x1, Pallas kernels, local(): pl.pallas_call(pack_kernel, in_specs=[ANY], out_specs=[VM] * 4, out_shape...  1.42 us
    pallas_call x1, Pallas kernels, local(): pl.pallas_call(band_kernel, in_specs=[VM] * 9, out_specs=VM, out_shape=sh...  0.97 us
  transfers between devices with their start and end apart: 11, of which 2 were waited for; matrix products, arithmetic and copies ran while one was open for 0% of the time, Pallas kernels for 40%

profile of v2, /device:TPU:1, one launch (start us, length us, event | category | flops | bytes accessed | tf_op | source)
XLA Modules:
  0.0 45.9 jit_solution(10565326967207385819)
XLA Ops:
  0.0 1.4 %pack.1 = (bf16[16,128,128]{2,1,0:T(8,128)(2,1)S(1)}, bf16[7,128,128]{2,1,0:T(8,128)(2,1)S(1)}, bf16[16,128,128]{2,1,0:T(8,128)(2,1)S(1)}, bf16[7,128,128]{2,1,0:T(8,128)(2,1)S(1)}) custom-call(bf16[2,13,128,128]{3,2,1,0:T(8,128)(2,1)} %density.5), custom_call_target="tpu_custom_call" | custom-call | tf_op jit(solution)/shard_map/pack/pallas_call | solution.py:301
  1.4 3.1 %collective-permute-start.4 = (bf16[16,128,128]{2,1,0:T(8,128)(2,1)S(1)}, bf16[16,128,128]{2,1,0:T(8,128)(2,1)S(1)}, u32[]{:S(2)}, u32[]{:S(2)}) collective-permute-start(bf16[16,128,128]{2,1,0:T(8,128)(2,1)S(1)} %get-tuple-element.23), channel_id=1, source_target_pairs={{4,8},{8,4},{12,16},{16,12},{20,24},{24,20},{28,32},{32,28},{36,40... | collective-permute-start | bytes 1572872 | tf_op jit(solution)/shard_map/ppermute | solution.py:39
  4.5 6.2 %collective-permute-start.6 = (bf16[16,128,128]{2,1,0:T(8,128)(2,1)S(1)}, bf16[16,128,128]{2,1,0:T(8,128)(2,1)S(1)}, u32[]{:S(2)}, u32[]{:S(2)}) collective-permute-start(bf16[16,128,128]{2,1,0:T(8,128)(2,1)S(1)} %get-tuple-element.25), channel_id=1, source_target_pairs={{0,4},{4,0},{8,12},{12,8},{16,20},{20,16},{24,28},{28,24},{32,36},... | collective-permute-start | bytes 1572872 | tf_op jit(solution)/shard_map/ppermute | solution.py:39
  10.8 0.7 %collective-permute-start.5 = (bf16[7,128,128]{2,1,0:T(8,128)(2,1)S(1)}, bf16[7,128,128]{2,1,0:T(8,128)(2,1)S(1)}, u32[]{:S(2)}, u32[]{:S(2)}) collective-permute-start(bf16[7,128,128]{2,1,0:T(8,128)(2,1)S(1)} %get-tuple-element.24), channel_id=1, source_target_pairs={{8,16},{16,8},{12,20},{20,12},{24,32},{32,24},{28,36},{36,28},{40,... | collective-permute-start | bytes 688136 | tf_op jit(solution)/shard_map/ppermute | solution.py:39
  11.5 0.0 collective-permute-start.7
  11.5 9.8 %cross.1 = (bf16[4,144,128]{2,1,0:T(8,128)(2,1)S(1)}, bf16[1,144,128]{2,1,0:T(8,128)(2,1)S(1)}, bf16[4,144,128]{2,1,0:T(8,128)(2,1)S(1)}, bf16[1,144,128]{2,1,0:...) custom-call(s32[2,4]{1,0:T(2,128)} %near_in.3, s32[2,4]{1,0:T(2,128)} %pick_in.3, ...), custom_call_target="tpu_custom_call" | custom-call | tf_op jit(solution)/shard_map/cross/pallas_call | solution.py:317
  21.3 0.9 %collective-permute-start = (bf16[4,144,128]{2,1,0:T(8,128)(2,1)S(1)}, bf16[4,144,128]{2,1,0:T(8,128)(2,1)S(1)}, u32[]{:S(2)}, u32[]{:S(2)}) collective-permute-start(bf16[4,144,128]{2,1,0:T(8,128)(2,1)S(1)} %get-tuple-element.18), channel_id=1, source_target_pairs={{4,8},{8,4},{12,16},{16,12},{20,24},{24,20},{28,32},{32,28},{36,40... | collective-permute-start | bytes 442376 | tf_op jit(solution)/shard_map/ppermute | solution.py:39
  22.2 0.0 collective-permute-done.5.far_d
  22.2 1.1 %collective-permute-start.2 = (bf16[4,144,128]{2,1,0:T(8,128)(2,1)S(1)}, bf16[4,144,128]{2,1,0:T(8,128)(2,1)S(1)}, u32[]{:S(2)}, u32[]{:S(2)}) collective-permute-start(bf16[4,144,128]{2,1,0:T(8,128)(2,1)S(1)} %get-tuple-element.20), channel_id=1, source_target_pairs={{0,4},{4,0},{8,12},{12,8},{16,20},{20,16},{24,28},{28,24},{32,36},... | collective-permute-start | bytes 442376 | tf_op jit(solution)/shard_map/ppermute | solution.py:39
  23.3 0.0 collective-permute-done.7.far_c
  23.3 4.6 %collective-permute-start.1 = (bf16[1,144,128]{2,1,0:T(8,128)(2,1)S(1)}, bf16[1,144,128]{2,1,0:T(8,128)(2,1)S(1)}, u32[]{:S(2)}, u32[]{:S(2)}) collective-permute-start(bf16[1,144,128]{2,1,0:T(8,128)(2,1)S(1)} %get-tuple-element.19), channel_id=1, source_target_pairs={{8,16},{16,8},{12,20},{20,12},{24,32},{32,24},{28,36},{36,28},{40,... | collective-permute-start | bytes 110600 | tf_op jit(solution)/shard_map/ppermute | solution.py:39
  27.9 0.0 collective-permute-done.4.far_b
  27.9 0.0 collective-permute-start.3
  27.9 0.0 collective-permute-done.6.far_a
  27.9 8.4 %own.1 = f32[2,128,128]{2,1,0:T(8,128)S(1)} custom-call(bf16[16,128,128]{2,1,0:T(8,128)(2,1)S(1)} %collective-permute-done.4.far_b, bf16[7,128,128]{2,1,0:T(8,128)(2,1)S(1)} %collective-permute-done.5.far_d, bf16[16,128,128]{2,1,0:T(8,128)(2,1)S(1)} %collective-permute-done.6.far_a, bf16[7,128,128]{2,1,0:T(8,128)(2,1)S(1)} %collective-permute-done.7.far_c, ...), custom_call_target="tpu_custom_call" | custom-call | tf_op jit(solution)/shard_map/own/pallas_call | solution.py:340
  36.4 0.0 collective-permute-done.1.in_d
  36.4 0.0 collective-permute-done.3.in_c
  36.4 0.0 collective-permute-done.in_b
  36.4 0.0 collective-permute-done.2.in_a
  36.4 1.3 %collective-permute-start.8 = (bf16[16,32,128]{2,1,0:T(8,128)(2,1)S(1)}, bf16[16,32,128]{2,1,0:T(8,128)(2,1)S(1)}, u32[]{:S(2)}, u32[]{:S(2)}) collective-permute-start(bf16[16,32,128]{2,1,0:T(8,128)(2,1)S(1)} %get-tuple-element.28), channel_id=1, source_target_pairs={{0,1},{1,2},{2,3},{3,0},{4,5},{5,6},{6,7},{7,4},{8,9},{9,10},{10,1... | collective-permute-start | bytes 393224 | tf_op jit(solution)/shard_map/ppermute | solution.py:363
  37.7 2.4 %collective-permute-start.9 = (bf16[16,32,128]{2,1,0:T(8,128)(2,1)S(1)}, bf16[16,32,128]{2,1,0:T(8,128)(2,1)S(1)}, u32[]{:S(2)}, u32[]{:S(2)}) collective-permute-start(bf16[16,32,128]{2,1,0:T(8,128)(2,1)S(1)} %get-tuple-element.29), channel_id=1, source_target_pairs={{0,2},{1,3},{2,0},{3,1},{4,6},{5,7},{6,4},{7,5},{8,10},{9,11},{10,... | collective-permute-start | bytes 393224 | tf_op jit(solution)/shard_map/ppermute | solution.py:363
  40.2 1.2 %collective-permute-start.10 = (bf16[16,32,128]{2,1,0:T(8,128)(2,1)S(1)}, bf16[16,32,128]{2,1,0:T(8,128)(2,1)S(1)}, u32[]{:S(2)}, u32[]{:S(2)}) collective-permute-start(bf16[16,32,128]{2,1,0:T(8,128)(2,1)S(1)} %get-tuple-element.30), channel_id=1, source_target_pairs={{0,3},{1,0},{2,1},{3,2},{4,7},{5,4},{6,5},{7,6},{8,11},{9,8},{10,9... | collective-permute-start | bytes 393224 | tf_op jit(solution)/shard_map/ppermute | solution.py:363
  41.3 1.9 %collective-permute-done.8.from_1 = bf16[16,32,128]{2,1,0:T(8,128)(2,1)S(1)} collective-permute-done((bf16[16,32,128]{2,1,0:T(8,128)(2,1)S(1)}, bf16[16,32,128]{2,1,0:T(8,128)(2,1)S(1)}, u32[]{:S(2)}, u32[]{:S(2)}) %collective-permute-start.8) | collective-permute-done | bytes 131104 | tf_op jit(solution)/shard_map/ppermute | solution.py:363
  43.2 1.7 %collective-permute-done.9.from_2 = bf16[16,32,128]{2,1,0:T(8,128)(2,1)S(1)} collective-permute-done((bf16[16,32,128]{2,1,0:T(8,128)(2,1)S(1)}, bf16[16,32,128]{2,1,0:T(8,128)(2,1)S(1)}, u32[]{:S(2)}, u32[]{:S(2)}) %collective-permute-start.9) | collective-permute-done | bytes 131104 | tf_op jit(solution)/shard_map/ppermute | solution.py:363
  44.9 0.0 collective-permute-done.10.from_3
  44.9 1.0 %band.1 = f32[26,32,128]{2,1,0:T(8,128)} custom-call(bf16[4,144,128]{2,1,0:T(8,128)(2,1)S(1)} %collective-permute-done.in_b, bf16[1,144,128]{2,1,0:T(8,128)(2,1)S(1)} %collective-permute-done.1.in_d, bf16[4,144,128]{2,1,0:T(8,128)(2,1)S(1)} %collective-permute-done.2.in_a, bf16[1,144,128]{2,1,0:T(8,128)(2,1)S(1)} %collective-permute-done.3.in_c, ...), custom_call_target="tpu_custom_call" | custom-call | tf_op jit(solution)/shard_map/band/pallas_call | solution.py:364
  (1 shorter events, 0.0 us)
Async XLA Ops:
  1.4 26.5 %collective-permute-start.4 = (bf16[16,128,128]{2,1,0:T(8,128)(2,1)S(1)}, bf16[16,128,128]{2,1,0:T(8,128)(2,1)S(1)}, u32[]{:S(2)}, u32[]{:S(2)}) collective-permute-start(bf16[16,128,128]{2,1,0:T(8,128)(2,1)S(1)} %get-tuple-element.23), channel_id=1, source_target_pairs={{4,8},{8,4},{12,16},{16,12},{20,24},{24,20},{28,32},{32,28},{36,40... | collective-permute-start | bytes 1572872 | tf_op jit(solution)/shard_map/ppermute | solution.py:39
  4.5 23.4 %collective-permute-start.6 = (bf16[16,128,128]{2,1,0:T(8,128)(2,1)S(1)}, bf16[16,128,128]{2,1,0:T(8,128)(2,1)S(1)}, u32[]{:S(2)}, u32[]{:S(2)}) collective-permute-start(bf16[16,128,128]{2,1,0:T(8,128)(2,1)S(1)} %get-tuple-element.25), channel_id=1, source_target_pairs={{0,4},{4,0},{8,12},{12,8},{16,20},{20,16},{24,28},{28,24},{32,36},... | collective-permute-start | bytes 1572872 | tf_op jit(solution)/shard_map/ppermute | solution.py:39
  10.8 11.4 %collective-permute-start.5 = (bf16[7,128,128]{2,1,0:T(8,128)(2,1)S(1)}, bf16[7,128,128]{2,1,0:T(8,128)(2,1)S(1)}, u32[]{:S(2)}, u32[]{:S(2)}) collective-permute-start(bf16[7,128,128]{2,1,0:T(8,128)(2,1)S(1)} %get-tuple-element.24), channel_id=1, source_target_pairs={{8,16},{16,8},{12,20},{20,12},{24,32},{32,24},{28,36},{36,28},{40,... | collective-permute-start | bytes 688136 | tf_op jit(solution)/shard_map/ppermute | solution.py:39
  11.5 11.8 %collective-permute-start.7 = (bf16[7,128,128]{2,1,0:T(8,128)(2,1)S(1)}, bf16[7,128,128]{2,1,0:T(8,128)(2,1)S(1)}, u32[]{:S(2)}, u32[]{:S(2)}) collective-permute-start(bf16[7,128,128]{2,1,0:T(8,128)(2,1)S(1)} %get-tuple-element.26), channel_id=1, source_target_pairs={{0,8},{8,0},{4,12},{12,4},{16,24},{24,16},{20,28},{28,20},{32,40},... | collective-permute-start | bytes 688136 | tf_op jit(solution)/shard_map/ppermute | solution.py:39
  21.3 15.1 %collective-permute-start = (bf16[4,144,128]{2,1,0:T(8,128)(2,1)S(1)}, bf16[4,144,128]{2,1,0:T(8,128)(2,1)S(1)}, u32[]{:S(2)}, u32[]{:S(2)}) collective-permute-start(bf16[4,144,128]{2,1,0:T(8,128)(2,1)S(1)} %get-tuple-element.18), channel_id=1, source_target_pairs={{4,8},{8,4},{12,16},{16,12},{20,24},{24,20},{28,32},{32,28},{36,40... | collective-permute-start | bytes 442376 | tf_op jit(solution)/shard_map/ppermute | solution.py:39
  22.2 14.2 %collective-permute-start.2 = (bf16[4,144,128]{2,1,0:T(8,128)(2,1)S(1)}, bf16[4,144,128]{2,1,0:T(8,128)(2,1)S(1)}, u32[]{:S(2)}, u32[]{:S(2)}) collective-permute-start(bf16[4,144,128]{2,1,0:T(8,128)(2,1)S(1)} %get-tuple-element.20), channel_id=1, source_target_pairs={{0,4},{4,0},{8,12},{12,8},{16,20},{20,16},{24,28},{28,24},{32,36},... | collective-permute-start | bytes 442376 | tf_op jit(solution)/shard_map/ppermute | solution.py:39
  23.3 13.1 %collective-permute-start.1 = (bf16[1,144,128]{2,1,0:T(8,128)(2,1)S(1)}, bf16[1,144,128]{2,1,0:T(8,128)(2,1)S(1)}, u32[]{:S(2)}, u32[]{:S(2)}) collective-permute-start(bf16[1,144,128]{2,1,0:T(8,128)(2,1)S(1)} %get-tuple-element.19), channel_id=1, source_target_pairs={{8,16},{16,8},{12,20},{20,12},{24,32},{32,24},{28,36},{36,28},{40,... | collective-permute-start | bytes 110600 | tf_op jit(solution)/shard_map/ppermute | solution.py:39
  27.9 8.4 %collective-permute-start.3 = (bf16[1,144,128]{2,1,0:T(8,128)(2,1)S(1)}, bf16[1,144,128]{2,1,0:T(8,128)(2,1)S(1)}, u32[]{:S(2)}, u32[]{:S(2)}) collective-permute-start(bf16[1,144,128]{2,1,0:T(8,128)(2,1)S(1)} %get-tuple-element.21), channel_id=1, source_target_pairs={{0,8},{8,0},{4,12},{12,4},{16,24},{24,16},{20,28},{28,20},{32,40},... | collective-permute-start | bytes 110600 | tf_op jit(solution)/shard_map/ppermute | solution.py:39
  36.4 6.8 %collective-permute-start.8 = (bf16[16,32,128]{2,1,0:T(8,128)(2,1)S(1)}, bf16[16,32,128]{2,1,0:T(8,128)(2,1)S(1)}, u32[]{:S(2)}, u32[]{:S(2)}) collective-permute-start(bf16[16,32,128]{2,1,0:T(8,128)(2,1)S(1)} %get-tuple-element.28), channel_id=1, source_target_pairs={{0,1},{1,2},{2,3},{3,0},{4,5},{5,6},{6,7},{7,4},{8,9},{9,10},{10,1... | collective-permute-start | bytes 393224 | tf_op jit(solution)/shard_map/ppermute | solution.py:363
  37.7 7.2 %collective-permute-start.9 = (bf16[16,32,128]{2,1,0:T(8,128)(2,1)S(1)}, bf16[16,32,128]{2,1,0:T(8,128)(2,1)S(1)}, u32[]{:S(2)}, u32[]{:S(2)}) collective-permute-start(bf16[16,32,128]{2,1,0:T(8,128)(2,1)S(1)} %get-tuple-element.29), channel_id=1, source_target_pairs={{0,2},{1,3},{2,0},{3,1},{4,6},{5,7},{6,4},{7,5},{8,10},{9,11},{10,... | collective-permute-start | bytes 393224 | tf_op jit(solution)/shard_map/ppermute | solution.py:363
  40.2 4.8 %collective-permute-start.10 = (bf16[16,32,128]{2,1,0:T(8,128)(2,1)S(1)}, bf16[16,32,128]{2,1,0:T(8,128)(2,1)S(1)}, u32[]{:S(2)}, u32[]{:S(2)}) collective-permute-start(bf16[16,32,128]{2,1,0:T(8,128)(2,1)S(1)} %get-tuple-element.30), channel_id=1, source_target_pairs={{0,3},{1,0},{2,1},{3,2},{4,7},{5,4},{6,5},{7,6},{8,11},{9,8},{10,9... | collective-permute-start | bytes 393224 | tf_op jit(solution)/shard_map/ppermute | solution.py:363

commit v3 on v2

--- a/solution.py
+++ b/solution.py
@@ -9,6 +9,7 @@
 SLAB = 8
 ROWS = 32
 EDGE = 16
+FLIGHT = 2
 f32 = jnp.float32
 bf16 = jnp.bfloat16
 VM = pl.BlockSpec(memory_space=pltpu.VMEM)
@@ -106,7 +107,9 @@
         return pl.when(jnp.logical_and(self.active, condition))
 
 
-def pack_kernel(density, out_b, out_d, out_a, out_c, sems):
+def pack_kernel(
+    density, near_in, pick_in, mask_in, out_b, out_d, out_a, out_c, near, pick, mask, sems
+):
     mine = lax.axis_index("sfc")
     plus_a = 1 - lax.rem(mine, 2)
     plus_c = 1 - lax.rem(mine, 4) // 2
@@ -116,6 +119,7 @@
         copies.append((density.at[1, pl.ds(4 * plus, 8)], ref.at[pl.ds(8, 8)]))
     for ref, plus in ((out_d, 1 - plus_c), (out_c, plus_c)):
         copies.append((density.at[plus, pl.ds(6 * plus, 7)], ref))
+    copies += [(near_in, near), (pick_in, pick), (mask_in, mask)]
     made = [pltpu.make_async_copy(s, d, sems.at[i]) for i, (s, d) in enumerate(copies)]
     for copy in made:
         copy.start()
@@ -131,79 +135,96 @@
 
 def cross_kernel(
     near_in, pick_in, mask_in, source, density,
-    out_b, out_d, out_a, out_c, inside, blocks,
-    near, pick, mask, home, held, int_sems, home_sem, sems,
-):
-    def loads(g):
-        return [
-            pltpu.make_async_copy(source.at[g, j], blocks.at[g, j], sems.at[g, j])
-            for j in range(4)
-        ]
-
-    center = pltpu.make_async_copy(density.at[:, 6], home, home_sem)
-    center.start()
-    for copy in loads(0):
-        copy.start()
-    fetch_ints((near_in, pick_in, mask_in), (near, pick, mask), int_sems)
-    for ref in (out_b, out_d, out_a, out_c, inside):
-        ref[...] = jnp.zeros_like(ref)
-    center.wait()
-
-    def visit(i, carry):
-        pair = Pair(i, near, pick, mask)
-        g, j, k, shift = pair.g, pair.j, pair.k, pair.shift
-
-        @pl.when(pair.active)
-        def _():
-            value = right_cross(home[g], blocks.at[g, k], blocks.at[g, j], held).astype(bf16)
-            slot = jnp.where(pair.reach > 0, 3 * g + shift - 2, g - shift - 1)
-            slot = jnp.clip(slot, 0, 3)
-
-            @pl.when(pair.reach == 0)
-            def _():
-                put(inside, jnp.clip(3 * g + shift, 0, 3), value, pair)
-
-            @pl.when(pair.in_a)
-            def _():
-                put(out_a, slot, value, pair)
-
-            @pl.when(pair.in_b)
-            def _():
-                put(out_b, slot, value, pair)
-
-            @pl.when(pair.in_c)
-            def _():
-                put(out_c, 0, value, pair)
-
-            @pl.when(pair.in_d)
-            def _():
-                put(out_d, 0, value, pair)
-
-        return carry
-
-    def group(g, carry):
-        for j in range(4):
-            pltpu.make_async_copy(source.at[0, 0], blocks.at[0, 0], sems.at[g, j]).wait()
-
-        @pl.when(g == 0)
-        def _():
-            for copy in loads(1):
-                copy.start()
-
-        return lax.fori_loop(4 * g, 4 * g + 4, visit, carry)
-
-    lax.fori_loop(0, 2, group, 0)
-
-
-def own_kernel(
-    far_b, far_d, far_a, far_c, near_in, pick_in, mask_in, blocks, density, own,
-    near, pick, mask, held, far, whole, int_sems, whole_sem,
+    out_b, out_d, out_a, out_c, inside, blocks, whole,
+    near, pick, mask, queue, state, upto, held, int_sems, whole_sem, sems,
 ):
     copy = pltpu.make_async_copy(density, whole, whole_sem)
     copy.start()
     fetch_ints((near_in, pick_in, mask_in), (near, pick, mask), int_sems)
+    for i in range(8):
+        state[i] = 0
+
+    def demand(t, length):
+        pair = Pair(t, near, pick, mask)
+        for other in (pair.k, pair.j):
+            index = 4 * pair.g + other
+            fresh = jnp.logical_and(state[index] == 0, pair.active)
+
+            @pl.when(fresh)
+            def _():
+                queue[length] = index
+                state[index] = 1
+
+            length = length + jnp.where(fresh, 1, 0)
+        upto[t] = length
+        return length
+
+    length = lax.fori_loop(0, 8, demand, 0)
+
+    def load(q, carry):
+        @pl.when(q < length)
+        def _():
+            index = queue[q]
+            g, j = index // 4, lax.rem(index, 4)
+            pltpu.make_async_copy(source.at[g, j], blocks.at[g, j], sems.at[index]).start()
+
+        return carry
+
+    def arrive(q, carry):
+        pltpu.make_async_copy(source.at[0, 0], blocks.at[0, 0], sems.at[queue[q]]).wait()
+        return load(q + FLIGHT, carry)
+
+    lax.fori_loop(0, FLIGHT, load, 0)
+    for ref in (out_b, out_d, out_a, out_c, inside):
+        ref[...] = jnp.zeros_like(ref)
+    copy.wait()
+
+    def store(pair, value):
+        value = value.astype(bf16)
+        g, shift = pair.g, pair.shift
+        slot = jnp.where(pair.reach > 0, 3 * g + shift - 2, g - shift - 1)
+        slot = jnp.clip(slot, 0, 3)
+
+        @pl.when(pair.reach == 0)
+        def _():
+            put(inside, jnp.clip(3 * g + shift, 0, 3), value, pair)
+
+        @pl.when(pair.in_a)
+        def _():
+            put(out_a, slot, value, pair)
+
+        @pl.when(pair.in_b)
+        def _():
+            put(out_b, slot, value, pair)
+
+        @pl.when(pair.in_c)
+        def _():
+            put(out_c, 0, value, pair)
+
+        @pl.when(pair.in_d)
+        def _():
+            put(out_d, 0, value, pair)
+
+    def visit(i, arrived):
+        pair = Pair(i, near, pick, mask)
+        g, j, k = pair.g, pair.j, pair.k
+        lax.fori_loop(arrived, upto[i], arrive, 0)
+
+        @pl.when(pair.active)
+        def _():
+            store(pair, right_cross(whole[g, 6], blocks.at[g, k], blocks.at[g, j], held))
+
+        return upto[i]
+
+    lax.fori_loop(0, 8, visit, 0)
+
+
+def own_kernel(
+    far_b, far_d, far_a, far_c, near_in, pick_in, mask_in, blocks, whole, own,
+    near, pick, mask, held, far, int_sems,
+):
+    fetch_ints((near_in, pick_in, mask_in), (near, pick, mask), int_sems)
     own[...] = jnp.zeros_like(own)
-    copy.wait()
 
     def visit(i, carry):
         pair = Pair(i, near, pick, mask)
@@ -242,13 +263,13 @@
     lax.fori_loop(0, 8, visit, 0)
 
 
-def rows_kernel(in_b, in_d, in_a, in_c, in_l, own, *outs):
+def rows_kernel(in_d, in_b, in_a, in_c, in_l, own, *outs):
     side = lax.axis_index("aux")
     for step, out in enumerate(outs):
         start = pl.multiple_of(lax.rem(side + step + 1, 4) * ROWS, ROWS)
         at = 0
         for ref in (in_b, in_d, in_a, in_c, in_l):
-            for slot in range(ref.shape[0]):
+            for slot in range(1 if ref is in_c or ref is in_d else 4):
                 out[at] = ref[slot, pl.ds(start, ROWS)]
                 at += 1
         for g in range(2):
@@ -256,7 +277,7 @@
             at += 1
 
 
-def band_kernel(in_b, in_d, in_a, in_c, in_l, own, from_1, from_2, from_3, band):
+def band_kernel(in_d, in_b, in_a, in_c, in_l, own, from_1, from_2, from_3, band):
     side = lax.axis_index("aux")
     start = pl.multiple_of(side * ROWS, ROWS)
     band[...] = jnp.zeros_like(band)
@@ -269,7 +290,7 @@
     at = 0
     found = []
     for ref in (in_b, in_d, in_a, in_c, in_l):
-        for slot in range(ref.shape[0]):
+        for slot in range(1 if ref is in_c or ref is in_d else 4):
             label = jnp.max(ref[slot, pl.ds(BASIS, EDGE)].astype(f32)).astype(jnp.int32)
             value = ref[slot, pl.ds(start, ROWS)].astype(f32) + others(at)
             found.append((jnp.clip(label, 0, 25), value))
@@ -300,13 +321,15 @@
     dma = pltpu.SemaphoreType.DMA
     packed = pl.pallas_call(
         pack_kernel,
-        in_specs=[ANY],
-        out_specs=[VM] * 4,
-        out_shape=[shape(16, 128, 128), shape(7, 128, 128), shape(16, 128, 128), shape(7, 128, 128)],
-        scratch_shapes=[dma((6,))],
+        in_specs=[ANY] * 4,
+        out_specs=[VM] * 7,
+        out_shape=[shape(n, 128, 128) for n in (16, 7, 16, 7)]
+        + [pltpu.VMEM((2, 4), jnp.int32)] * 3,
+        scratch_shapes=[dma((9,))],
         compiler_params=small,
         name="pack",
-    )(density)
+    )(density, *ints)
+    ints = packed[4:]
     far_b = swapped(packed[0], "b")
     far_d = swapped(packed[1], "d")
     far_a = swapped(packed[2], "a")
@@ -314,21 +337,22 @@
 
     tall = BASIS + EDGE
     held = pltpu.VMEM((40 * BASIS, BASIS), bf16)
-    out_b, out_d, out_a, out_c, inside, blocks = pl.pallas_call(
+    out_b, out_d, out_a, out_c, inside, blocks, whole = pl.pallas_call(
         cross_kernel,
         in_specs=[ANY] * 5,
-        out_specs=[VM] * 6,
+        out_specs=[VM] * 7,
         out_shape=[
             shape(4, tall, 128),
-            shape(1, tall, 128),
             shape(4, tall, 128),
-            shape(1, tall, 128),
+            shape(4, tall, 128),
+            shape(4, tall, 128),
             shape(4, tall, 128),
             pltpu.VMEM(three_index.shape, bf16),
+            pltpu.VMEM(density.shape, bf16),
         ],
         scratch_shapes=int_scratch()
-        + [pltpu.VMEM((2, 128, 128), bf16), held]
-        + [dma((3,)), dma(()), dma((2, 4))],
+        + [pltpu.SMEM((8,), jnp.int32)] * 3
+        + [held, dma((3,)), dma(()), dma((8,))],
         compiler_params=limit,
         name="cross",
     )(*ints, three_index, density)
@@ -339,16 +363,15 @@
 
     own = pl.pallas_call(
         own_kernel,
-        in_specs=[VM] * 4 + [ANY] * 3 + [VM, ANY],
+        in_specs=[VM] * 4 + [ANY] * 3 + [VM, VM],
         out_specs=VM,
         out_shape=shape(2, 128, 128, dtype=f32),
-        scratch_shapes=int_scratch()
-        + [held, pltpu.VMEM((128, 128), bf16), pltpu.VMEM(density.shape, bf16), dma((3,)), dma(())],
+        scratch_shapes=int_scratch() + [held, pltpu.VMEM((128, 128), bf16), dma((3,))],
         compiler_params=limit,
         name="own",
-    )(far_b, far_d, far_a, far_c, *ints, blocks, density)
-
-    arrived = (in_b, in_d, in_a, in_c, inside, own)
+    )(far_b, far_d, far_a, far_c, *ints, blocks, whole)
+
+    arrived = (in_d, in_b, in_a, in_c, inside, own)
     sends = pl.pallas_call(
         rows_kernel,
         in_specs=[VM] * 6,

time: 45.6 us -> 43.5 us (0.954)
  the two profiles are of different devices: /device:TPU:1 before, /device:TPU:6 now
where the time goes in v3:
time: 43.5 us; the launch traced here: 43.3 us
  starting transfers between devices  21 us (48%)
  Pallas kernels  15.3 us (35%)
  waiting for transfers between devices  6.92 us (16%)
    ppermute x8, starting transfers between devices, swapped(): return lax.ppermute(value, 'sfc', pairs)  18.1 us
    pallas_call x1, Pallas kernels, local(): pl.pallas_call(cross_kernel, in_specs=[ANY] * 5, out_specs=[VM] * 7, out_...  7.5 us
    ppermute x3, waiting for transfers between devices, local(): received.append(lax.ppermute(send, 'aux', pairs))  6.17 us
    pallas_call x1, Pallas kernels, local(): pl.pallas_call(own_kernel, in_specs=[VM] * 4 + [ANY] * 3 + [VM, VM], out_...  5.36 us
    ppermute x3, starting transfers between devices, local(): received.append(lax.ppermute(send, 'aux', pairs))  2.98 us
    pallas_call x1, Pallas kernels, local(): pl.pallas_call(pack_kernel, in_specs=[ANY] * 4, out_specs=[VM] * 7, out_s...  1.44 us
    pallas_call x1, Pallas kernels, local(): pl.pallas_call(band_kernel, in_specs=[VM] * 9, out_specs=VM, out_shape=sh...  0.97 us
  transfers between devices with their start and end apart: 11, of which 4 were waited for; matrix products, arithmetic and copies ran while one was open for 0% of the time, Pallas kernels for 30%

profile of v3, /device:TPU:6, one launch (start us, length us, event | category | flops | bytes accessed | tf_op | source)
XLA Modules:
  0.0 43.3 jit_solution(2533617827594007752)
XLA Ops:
  0.0 1.4 %pack.1 = (bf16[16,128,128]{2,1,0:T(8,128)(2,1)S(1)}, bf16[7,128,128]{2,1,0:T(8,128)(2,1)S(1)}, bf16[16,128,128]{2,1,0:T(8,128)(2,1)S(1)}, bf16[7,128,128]{2,1,0...) custom-call(bf16[2,13,128,128]{3,2,1,0:T(8,128)(2,1)} %density.3, s32[2,4]{1,0:T(2,128)} %near_in.1, ...), custom_call_target="tpu_custom_call" | custom-call | tf_op jit(solution)/shard_map/pack/pallas_call | solution.py:322
  1.4 7.8 %collective-permute-start.4 = (bf16[16,128,128]{2,1,0:T(8,128)(2,1)S(1)}, bf16[16,128,128]{2,1,0:T(8,128)(2,1)S(1)}, u32[]{:S(2)}, u32[]{:S(2)}) collective-permute-start(bf16[16,128,128]{2,1,0:T(8,128)(2,1)S(1)} %get-tuple-element.30), channel_id=1, source_target_pairs={{4,8},{8,4},{12,16},{16,12},{20,24},{24,20},{28,32},{32,28},{36,40... | collective-permute-start | bytes 1572872 | tf_op jit(solution)/shard_map/ppermute | solution.py:40
  9.3 0.0 collective-permute-start.6
  9.3 1.0 %collective-permute-start.5 = (bf16[7,128,128]{2,1,0:T(8,128)(2,1)S(1)}, bf16[7,128,128]{2,1,0:T(8,128)(2,1)S(1)}, u32[]{:S(2)}, u32[]{:S(2)}) collective-permute-start(bf16[7,128,128]{2,1,0:T(8,128)(2,1)S(1)} %get-tuple-element.31), channel_id=1, source_target_pairs={{8,16},{16,8},{12,20},{20,12},{24,32},{32,24},{28,36},{36,28},{40,... | collective-permute-start | bytes 688136 | tf_op jit(solution)/shard_map/ppermute | solution.py:40
  10.3 0.0 collective-permute-start.7
  10.3 7.5 %cross.1 = (bf16[4,144,128]{2,1,0:T(8,128)(2,1)S(1)}, bf16[4,144,128]{2,1,0:T(8,128)(2,1)S(1)}, bf16[4,144,128]{2,1,0:T(8,128)(2,1)S(1)}, bf16[4,144,128]{2,1,0:...) custom-call(s32[2,4]{1,0:T(2,128)S(1)} %get-tuple-element.22.near_in, ...), custom_call_target="tpu_custom_call" | custom-call | tf_op jit(solution)/shard_map/cross/pallas_call | solution.py:340
  17.8 4.4 %collective-permute-start = (bf16[4,144,128]{2,1,0:T(8,128)(2,1)S(1)}, bf16[4,144,128]{2,1,0:T(8,128)(2,1)S(1)}, u32[]{:S(2)}, u32[]{:S(2)}) collective-permute-start(bf16[4,144,128]{2,1,0:T(8,128)(2,1)S(1)} %get-tuple-element.25), channel_id=1, source_target_pairs={{8,16},{16,8},{12,20},{20,12},{24,32},{32,24},{28,36},{36,28},{40,... | collective-permute-start | bytes 442376 | tf_op jit(solution)/shard_map/ppermute | solution.py:40
  22.2 0.0 collective-permute-done.5.far_d
  22.2 3.1 %collective-permute-start.1 = (bf16[4,144,128]{2,1,0:T(8,128)(2,1)S(1)}, bf16[4,144,128]{2,1,0:T(8,128)(2,1)S(1)}, u32[]{:S(2)}, u32[]{:S(2)}) collective-permute-start(bf16[4,144,128]{2,1,0:T(8,128)(2,1)S(1)} %get-tuple-element.26), channel_id=1, source_target_pairs={{4,8},{8,4},{12,16},{16,12},{20,24},{24,20},{28,32},{32,28},{36,40... | collective-permute-start | bytes 442376 | tf_op jit(solution)/shard_map/ppermute | solution.py:40
  25.3 0.0 collective-permute-done.7.far_c
  25.3 0.1 collective-permute-start.2
  25.4 0.0 collective-permute-done.4.far_b
  25.4 1.6 %collective-permute-start.3 = (bf16[4,144,128]{2,1,0:T(8,128)(2,1)S(1)}, bf16[4,144,128]{2,1,0:T(8,128)(2,1)S(1)}, u32[]{:S(2)}, u32[]{:S(2)}) collective-permute-start(bf16[4,144,128]{2,1,0:T(8,128)(2,1)S(1)} %get-tuple-element.28), channel_id=1, source_target_pairs={{0,8},{8,0},{4,12},{12,4},{16,24},{24,16},{20,28},{28,20},{32,40},... | collective-permute-start | bytes 442376 | tf_op jit(solution)/shard_map/ppermute | solution.py:40
  27.0 0.0 collective-permute-done.6.far_a
  27.0 5.4 %own.1 = f32[2,128,128]{2,1,0:T(8,128)S(1)} custom-call(bf16[16,128,128]{2,1,0:T(8,128)(2,1)S(1)} %collective-permute-done.4.far_b, bf16[7,128,128]{2,1,0:T(8,128)(2,1)S(1)} %collective-permute-done.5.far_d, bf16[16,128,128]{2,1,0:T(8,128)(2,1)S(1)} %collective-permute-done.6.far_a, bf16[7,128,128]{2,1,0:T(8,128)(2,1)S(1)} %collective-permute-done.7.far_c, ...), custom_call_target="tpu_custom_call" | custom-call | tf_op jit(solution)/shard_map/own/pallas_call | solution.py:364
  32.4 0.0 collective-permute-done.in_d
  32.4 0.0 collective-permute-done.1.in_b
  32.4 0.0 collective-permute-done.2.in_a
  32.4 0.7 %collective-permute-done.3.in_c = bf16[4,144,128]{2,1,0:T(8,128)(2,1)S(1)} collective-permute-done((bf16[4,144,128]{2,1,0:T(8,128)(2,1)S(1)}, bf16[4,144,128]{2,1,0:T(8,128)(2,1)S(1)}, u32[]{:S(2)}, u32[]{:S(2)}) %collective-permute-start.3) | collective-permute-done | bytes 147488 | tf_op jit(solution)/shard_map/ppermute | solution.py:40
  33.2 0.6 %collective-permute-start.8 = (bf16[16,32,128]{2,1,0:T(8,128)(2,1)S(1)}, bf16[16,32,128]{2,1,0:T(8,128)(2,1)S(1)}, u32[]{:S(2)}, u32[]{:S(2)}) collective-permute-start(bf16[16,32,128]{2,1,0:T(8,128)(2,1)S(1)} %get-tuple-element.36), channel_id=1, source_target_pairs={{0,1},{1,2},{2,3},{3,0},{4,5},{5,6},{6,7},{7,4},{8,9},{9,10},{10,1... | collective-permute-start | bytes 393224 | tf_op jit(solution)/shard_map/ppermute | solution.py:386
  33.7 2.4 %collective-permute-start.9 = (bf16[16,32,128]{2,1,0:T(8,128)(2,1)S(1)}, bf16[16,32,128]{2,1,0:T(8,128)(2,1)S(1)}, u32[]{:S(2)}, u32[]{:S(2)}) collective-permute-start(bf16[16,32,128]{2,1,0:T(8,128)(2,1)S(1)} %get-tuple-element.37), channel_id=1, source_target_pairs={{0,2},{1,3},{2,0},{3,1},{4,6},{5,7},{6,4},{7,5},{8,10},{9,11},{10,... | collective-permute-start | bytes 393224 | tf_op jit(solution)/shard_map/ppermute | solution.py:386
  36.2 0.0 collective-permute-start.10
  36.2 2.2 %collective-permute-done.8.from_1 = bf16[16,32,128]{2,1,0:T(8,128)(2,1)S(1)} collective-permute-done((bf16[16,32,128]{2,1,0:T(8,128)(2,1)S(1)}, bf16[16,32,128]{2,1,0:T(8,128)(2,1)S(1)}, u32[]{:S(2)}, u32[]{:S(2)}) %collective-permute-start.8) | collective-permute-done | bytes 131104 | tf_op jit(solution)/shard_map/ppermute | solution.py:386
  38.3 2.2 %collective-permute-done.9.from_2 = bf16[16,32,128]{2,1,0:T(8,128)(2,1)S(1)} collective-permute-done((bf16[16,32,128]{2,1,0:T(8,128)(2,1)S(1)}, bf16[16,32,128]{2,1,0:T(8,128)(2,1)S(1)}, u32[]{:S(2)}, u32[]{:S(2)}) %collective-permute-start.9) | collective-permute-done | bytes 131104 | tf_op jit(solution)/shard_map/ppermute | solution.py:386
  40.5 1.8 %collective-permute-done.10.from_3 = bf16[16,32,128]{2,1,0:T(8,128)(2,1)S(1)} collective-permute-done((bf16[16,32,128]{2,1,0:T(8,128)(2,1)S(1)}, bf16[16,32,128]{2,1,0:T(8,128)(2,1)S(1)}, u32[]{:S(2)}, u32[]{:S(2)}) %collective-permute-start.10) | collective-permute-done | bytes 131104 | tf_op jit(solution)/shard_map/ppermute | solution.py:386
  42.3 1.0 %band.1 = f32[26,32,128]{2,1,0:T(8,128)} custom-call(bf16[4,144,128]{2,1,0:T(8,128)(2,1)S(1)} %collective-permute-done.in_d, bf16[4,144,128]{2,1,0:T(8,128)(2,1)S(1)} %collective-permute-done.1.in_b, bf16[4,144,128]{2,1,0:T(8,128)(2,1)S(1)} %collective-permute-done.2.in_a, bf16[4,144,128]{2,1,0:T(8,128)(2,1)S(1)} %collective-permute-done.3.in_c, ...), custom_call_target="tpu_custom_call" | custom-call | tf_op jit(solution)/shard_map/band/pallas_call | solution.py:387
  (1 shorter events, 0.0 us)
Async XLA Ops:
  1.4 23.9 %collective-permute-start.4 = (bf16[16,128,128]{2,1,0:T(8,128)(2,1)S(1)}, bf16[16,128,128]{2,1,0:T(8,128)(2,1)S(1)}, u32[]{:S(2)}, u32[]{:S(2)}) collective-permute-start(bf16[16,128,128]{2,1,0:T(8,128)(2,1)S(1)} %get-tuple-element.30), channel_id=1, source_target_pairs={{4,8},{8,4},{12,16},{16,12},{20,24},{24,20},{28,32},{32,28},{36,40... | collective-permute-start | bytes 1572872 | tf_op jit(solution)/shard_map/ppermute | solution.py:40
  9.3 17.7 %collective-permute-start.6 = (bf16[16,128,128]{2,1,0:T(8,128)(2,1)S(1)}, bf16[16,128,128]{2,1,0:T(8,128)(2,1)S(1)}, u32[]{:S(2)}, u32[]{:S(2)}) collective-permute-start(bf16[16,128,128]{2,1,0:T(8,128)(2,1)S(1)} %get-tuple-element.32), channel_id=1, source_target_pairs={{0,4},{4,0},{8,12},{12,8},{16,20},{20,16},{24,28},{28,24},{32,36},... | collective-permute-start | bytes 1572872 | tf_op jit(solution)/shard_map/ppermute | solution.py:40
  9.3 12.9 %collective-permute-start.5 = (bf16[7,128,128]{2,1,0:T(8,128)(2,1)S(1)}, bf16[7,128,128]{2,1,0:T(8,128)(2,1)S(1)}, u32[]{:S(2)}, u32[]{:S(2)}) collective-permute-start(bf16[7,128,128]{2,1,0:T(8,128)(2,1)S(1)} %get-tuple-element.31), channel_id=1, source_target_pairs={{8,16},{16,8},{12,20},{20,12},{24,32},{32,24},{28,36},{36,28},{40,... | collective-permute-start | bytes 688136 | tf_op jit(solution)/shard_map/ppermute | solution.py:40
  10.3 15.0 %collective-permute-start.7 = (bf16[7,128,128]{2,1,0:T(8,128)(2,1)S(1)}, bf16[7,128,128]{2,1,0:T(8,128)(2,1)S(1)}, u32[]{:S(2)}, u32[]{:S(2)}) collective-permute-start(bf16[7,128,128]{2,1,0:T(8,128)(2,1)S(1)} %get-tuple-element.33), channel_id=1, source_target_pairs={{0,8},{8,0},{4,12},{12,4},{16,24},{24,16},{20,28},{28,20},{32,40},... | collective-permute-start | bytes 688136 | tf_op jit(solution)/shard_map/ppermute | solution.py:40
  17.8 14.6 %collective-permute-start = (bf16[4,144,128]{2,1,0:T(8,128)(2,1)S(1)}, bf16[4,144,128]{2,1,0:T(8,128)(2,1)S(1)}, u32[]{:S(2)}, u32[]{:S(2)}) collective-permute-start(bf16[4,144,128]{2,1,0:T(8,128)(2,1)S(1)} %get-tuple-element.25), channel_id=1, source_target_pairs={{8,16},{16,8},{12,20},{20,12},{24,32},{32,24},{28,36},{36,28},{40,... | collective-permute-start | bytes 442376 | tf_op jit(solution)/shard_map/ppermute | solution.py:40
  22.2 10.2 %collective-permute-start.1 = (bf16[4,144,128]{2,1,0:T(8,128)(2,1)S(1)}, bf16[4,144,128]{2,1,0:T(8,128)(2,1)S(1)}, u32[]{:S(2)}, u32[]{:S(2)}) collective-permute-start(bf16[4,144,128]{2,1,0:T(8,128)(2,1)S(1)} %get-tuple-element.26), channel_id=1, source_target_pairs={{4,8},{8,4},{12,16},{16,12},{20,24},{24,20},{28,32},{32,28},{36,40... | collective-permute-start | bytes 442376 | tf_op jit(solution)/shard_map/ppermute | solution.py:40
  25.3 7.1 %collective-permute-start.2 = (bf16[4,144,128]{2,1,0:T(8,128)(2,1)S(1)}, bf16[4,144,128]{2,1,0:T(8,128)(2,1)S(1)}, u32[]{:S(2)}, u32[]{:S(2)}) collective-permute-start(bf16[4,144,128]{2,1,0:T(8,128)(2,1)S(1)} %get-tuple-element.27), channel_id=1, source_target_pairs={{0,4},{4,0},{8,12},{12,8},{16,20},{20,16},{24,28},{28,24},{32,36},... | collective-permute-start | bytes 442376 | tf_op jit(solution)/shard_map/ppermute | solution.py:40
  25.4 7.8 %collective-permute-start.3 = (bf16[4,144,128]{2,1,0:T(8,128)(2,1)S(1)}, bf16[4,144,128]{2,1,0:T(8,128)(2,1)S(1)}, u32[]{:S(2)}, u32[]{:S(2)}) collective-permute-start(bf16[4,144,128]{2,1,0:T(8,128)(2,1)S(1)} %get-tuple-element.28), channel_id=1, source_target_pairs={{0,8},{8,0},{4,12},{12,4},{16,24},{24,16},{20,28},{28,20},{32,40},... | collective-permute-start | bytes 442376 | tf_op jit(solution)/shard_map/ppermute | solution.py:40
  33.2 5.1 %collective-permute-start.8 = (bf16[16,32,128]{2,1,0:T(8,128)(2,1)S(1)}, bf16[16,32,128]{2,1,0:T(8,128)(2,1)S(1)}, u32[]{:S(2)}, u32[]{:S(2)}) collective-permute-start(bf16[16,32,128]{2,1,0:T(8,128)(2,1)S(1)} %get-tuple-element.36), channel_id=1, source_target_pairs={{0,1},{1,2},{2,3},{3,0},{4,5},{5,6},{6,7},{7,4},{8,9},{9,10},{10,1... | collective-permute-start | bytes 393224 | tf_op jit(solution)/shard_map/ppermute | solution.py:386
  33.7 6.8 %collective-permute-start.9 = (bf16[16,32,128]{2,1,0:T(8,128)(2,1)S(1)}, bf16[16,32,128]{2,1,0:T(8,128)(2,1)S(1)}, u32[]{:S(2)}, u32[]{:S(2)}) collective-permute-start(bf16[16,32,128]{2,1,0:T(8,128)(2,1)S(1)} %get-tuple-element.37), channel_id=1, source_target_pairs={{0,2},{1,3},{2,0},{3,1},{4,6},{5,7},{6,4},{7,5},{8,10},{9,11},{10,... | collective-permute-start | bytes 393224 | tf_op jit(solution)/shard_map/ppermute | solution.py:386
  36.2 6.2 %collective-permute-start.10 = (bf16[16,32,128]{2,1,0:T(8,128)(2,1)S(1)}, bf16[16,32,128]{2,1,0:T(8,128)(2,1)S(1)}, u32[]{:S(2)}, u32[]{:S(2)}) collective-permute-start(bf16[16,32,128]{2,1,0:T(8,128)(2,1)S(1)} %get-tuple-element.38), channel_id=1, source_target_pairs={{0,3},{1,0},{2,1},{3,2},{4,7},{5,4},{6,5},{7,6},{8,11},{9,8},{10,9... | collective-permute-start | bytes 393224 | tf_op jit(solution)/shard_map/ppermute | solution.py:386
